TPU v7x, 128 devices: a whole 4x4x4 slice. The times are simulated.
128 devices in a mesh: node: 16 (over x, y), local: 8 (over z, core).
Axes of the slice: x: 4, y: 4, z: 4, core: 2. Of those that a mesh axis runs over, the one named last changes fastest.
Arguments:
- tokens: bfloat16 [16384, 4096], P(('node', 'local')), may hold values from -6 to 6
- expert_ids: int32 [16384, 8], P(('node', 'local')), may hold values from 0 to 127, all different within a row; in each aligned block of 128 rows (0 to 127, 128 to 255, ...) at most 10 rows name the same one
- route_probs: float32 [16384, 8], P(('node', 'local')), may hold values from 0.02 to 0.4
- cotangent: bfloat16 [16384, 4096], P(('node', 'local')), may hold values from -0.29882812 to 0.29882812
- gate_weight: bfloat16 [128, 4096, 768], P(('node', 'local')), may hold values from -0.09375 to 0.09375
- up_weight: bfloat16 [128, 4096, 768], P(('node', 'local')), may hold values from -0.09375 to 0.09375
- down_weight: bfloat16 [128, 768, 4096], P(('node', 'local')), may hold values from -0.21875 to 0.21875
Outputs:
- mixed_out: bfloat16 [16384, 4096], P(('node', 'local'))
- prob_grads: float32 [16384, 8], P(('node', 'local'))
Inputs may be any that keep to these rules, and one draw needn't show every extreme that they name: `expert_ids`: each row names 8 different experts. No expert is named by more than 10 of the rows of one device, a bound that some block reaches.
All inputs are finite; a program needn't handle non-finite values.
Results may differ from a plain program's by a relative error of at most 0.0058.
Values may be sent and summed in bfloat16 or wider, within the bound.
No kernel may reach another device: no remote copies, remote signals or barrier semaphores. Data moves between devices by JAX's collectives and lax.ppermute only.
A program may use at most 192 MiB of HBM per device.

v0:
```python
import jax
import jax.numpy as jnp
from jax import lax
from jax.sharding import PartitionSpec as P


def expert_apply(token_rows, gate_mat, up_mat, down_mat):
    gate_act = jnp.dot(token_rows, gate_mat, preferred_element_type=jnp.float32)
    up_act = jnp.dot(token_rows, up_mat, preferred_element_type=jnp.float32)
    hidden = (jax.nn.silu(gate_act) * up_act).astype(jnp.bfloat16)
    return jnp.dot(hidden, down_mat, preferred_element_type=jnp.float32).astype(jnp.bfloat16)


def per_device(tokens, expert_ids, route_probs, cotangent, gate_weight, up_weight, down_weight):
    tok_count, top_count = expert_ids.shape
    model_width = tokens.shape[1]
    node_count = lax.axis_size("node")
    local_count = lax.axis_size("local")
    expert_count = node_count * local_count
    capacity = max(2, tok_count * top_count * 5 // (4 * expert_count))
    slot_total = expert_count * capacity
    pair_experts = expert_ids.reshape(-1)
    expert_range = jnp.arange(expert_count, dtype=jnp.int32)
    one_hot = (pair_experts[:, None] == expert_range[None, :]).astype(jnp.int32)
    rank_in = jnp.sum((jnp.cumsum(one_hot, axis=0) - one_hot) * one_hot, axis=1)
    slot_ids = pair_experts * capacity + rank_in
    pair_tokens = jnp.arange(tok_count * top_count, dtype=jnp.int32) // top_count
    outgoing = (
        jnp.zeros((slot_total, model_width), jnp.bfloat16).at[slot_ids].set(tokens[pair_tokens])
    )
    outgoing = outgoing.reshape(expert_count, capacity, model_width)
    gate_mat = gate_weight[0]
    up_mat = up_weight[0]
    down_mat = down_weight[0]
    received = lax.all_to_all(outgoing, ("node", "local"), split_axis=0, concat_axis=0, tiled=True)
    results = expert_apply(received.reshape(slot_total, model_width), gate_mat, up_mat, down_mat)
    results = results.reshape(expert_count, capacity, model_width)
    returned = lax.all_to_all(results, ("node", "local"), split_axis=0, concat_axis=0, tiled=True)
    pair_out = returned.reshape(slot_total, model_width)[slot_ids].reshape(
        tok_count, top_count, model_width
    )
    mixed_out = jnp.sum(route_probs[:, :, None] * pair_out.astype(jnp.float32), axis=1).astype(
        jnp.bfloat16
    )
    prob_grads = jnp.einsum("td,tkd->tk", cotangent, pair_out, preferred_element_type=jnp.float32)
    return (mixed_out, prob_grads)


def solution(mesh):
    placed = (
        P(("node", "local"), None),
        P(("node", "local"), None),
        P(("node", "local"), None),
        P(("node", "local"), None),
        P(("node", "local"), None, None),
        P(("node", "local"), None, None),
        P(("node", "local"), None, None),
    )
    return jax.shard_map(
        per_device,
        mesh=mesh,
        in_specs=placed,
        out_specs=(P(("node", "local"), None), P(("node", "local"), None)),
        check_vma=False,
    )
```

profile of v0, /device:TPU:66, one launch (start us, length us, event | category | flops | bytes accessed | tf_op | source)
XLA Modules:
  0.0 626.7 jit_solution(5167973730640741386)
XLA Ops:
  0.6 0.9 copy.12
  1.7 0.7 broadcast_multiply_fusion
  2.4 0.1 copy.14
  2.5 0.2 fusion.18
  2.8 0.1 copy.15
  2.9 0.1 copy.11
  3.1 0.4 fusion.17
  3.5 7.7 %gather_fusion = bf16[1024,4096]{1,0:T(8,128)(2,1)} fusion(bf16[128,4096]{1,0:T(8,128)(2,1)S(1)} %copy-done, s32[1024]{0:T(1024)S(1)} %broadcast_clamp_fusion.1), kind=kCustom, calls=%fused_computation | custom fusion | bytes 16781312 | tf_op jit(solution)/shard_map/gather | solution.py:29
  11.3 19.0 %scatter_custom_fusion = bf16[1280,4096]{1,0:T(8,128)(2,1)} fusion(s32[1024]{0:T(1024)S(1)} %bitcast.36, bf16[1024,4096]{1,0:T(8,128)(2,1)} %gather_fusion, bf16[]{:T(256)} %constant.26.clone.1), kind=kCustom, calls=%fused_computation.12 | custom fusion | bytes 10486272 | tf_op jit(solution)/shard_map/scatter | solution.py:29
  30.2 15.2 %reshape.110 = bf16[128,10,4096]{2,1,0:T(8,128)(2,1)} reshape(bf16[1280,4096]{1,0:T(8,128)(2,1)} %scatter_custom_fusion) | data formatting | bytes 20971520 | tf_op jit(solution)/shard_map/reshape | solution.py:31
  45.4 199.4 %all_to_all.10 = bf16[128,10,4096]{2,1,0:T(8,128)(2,1)} all-to-all(bf16[128,10,4096]{2,1,0:T(8,128)(2,1)} %reshape.110), channel_id=1, replica_groups=mesh['node'=16,'local'=8] {'node','local'}, dimensions={0} | all-to-all | bytes 20971520 | tf_op jit(solution)/shard_map/all_to_all | solution.py:35
  244.9 16.5 %reshape.111 = bf16[1280,4096]{1,0:T(8,128)(2,1)} reshape(bf16[128,10,4096]{2,1,0:T(8,128)(2,1)} %all_to_all.10) | data formatting | bytes 20971520 | tf_op jit(solution)/shard_map/reshape | solution.py:36
  261.4 12.3 %fusion.5 = f32[1280,768]{1,0:T(8,128)S(1)} fusion(bf16[1280,4096]{1,0:T(8,128)(2,1)} %reshape.111, bf16[1,4096,768]{2,1,0:T(8,128)(2,1)} %param.11), kind=kOutput, calls=%fused_computation.10 | convolution fusion | flops 8053063680 | bytes 20709376 | tf_op jit(solution)/shard_map/dot_general | solution.py:8
  273.7 11.2 %fusion.12 = bf16[1280,768]{1,0:T(8,128)(2,1)S(1)} fusion(bf16[1280,4096]{1,0:T(8,128)(2,1)S(1)} %copy-done.2, bf16[1,4096,768]{2,1,0:T(8,128)(2,1)} %param.12, f32[1280,768]{1,0:T(8,128)S(1)} %fusion.5), kind=kOutput, calls=%fused_computation.15 | convolution fusion | flops 8058961920 | bytes 22675456 | tf_op jit(solution)/shard_map/dot_general | solution.py:9
  284.9 13.5 %convolution_convert_fusion = bf16[1280,4096]{1,0:T(8,128)(2,1)} fusion(bf16[1280,768]{1,0:T(8,128)(2,1)S(1)} %fusion.12, bf16[1,768,4096]{2,1,0:T(8,128)(2,1)} %param.13), kind=kOutput, calls=%fused_computation.4 | convolution fusion | flops 8058306560 | bytes 18743296 | tf_op jit(solution)/shard_map/dot_general | solution.py:11
  298.4 15.2 %reshape.112 = bf16[128,10,4096]{2,1,0:T(8,128)(2,1)} reshape(bf16[1280,4096]{1,0:T(8,128)(2,1)} %convolution_convert_fusion) | data formatting | bytes 20971520 | tf_op jit(solution)/shard_map/reshape | solution.py:37
  313.6 13.1 %all-to-all-start.1 = ((bf16[128,10,4096]{2,1,0:T(8,128)(2,1)}), bf16[128,10,4096]{2,1,0:T(8,128)(2,1)}, u32[]{:S(2)}, u32[]{:S(2)}) async-start(bf16[128,10,4096]{2,1,0:T(8,128)(2,1)} %reshape.112), calls=%async_computation.1 | async-start | bytes 33554432 | tf_op jit(solution)/shard_map/all_to_all | solution.py:38
  326.7 0.1 copy.10
  326.8 240.1 %all-to-all-done.1 = bf16[128,10,4096]{2,1,0:T(8,128)(2,1)} async-done(((bf16[128,10,4096]{2,1,0:T(8,128)(2,1)}), bf16[128,10,4096]{2,1,0:T(8,128)(2,1)}, u32[]{:S(2)}, u32[]{:S(2)}) %all-to-all-start.1) | async-done | bytes 10485792 | tf_op jit(solution)/shard_map/all_to_all | solution.py:38
  566.9 16.5 %reshape.113 = bf16[1280,4096]{1,0:T(8,128)(2,1)} reshape(bf16[128,10,4096]{2,1,0:T(8,128)(2,1)} %all-to-all-done.1) | data formatting | bytes 20971520 | tf_op jit(solution)/shard_map/reshape | solution.py:39
  583.4 20.4 %gather_fusion.1 = bf16[1024,4096]{1,0:T(8,128)(2,1)} fusion(bf16[1280,4096]{1,0:T(8,128)(2,1)} %reshape.113, s32[1024]{0:T(1024)S(1)} %broadcast_clamp_fusion), kind=kCustom, calls=%fused_computation.1 | custom fusion | bytes 16781312 | tf_op jit(solution)/shard_map/gather | solution.py:39
  603.8 13.0 %multiply_reduce_fusion = bf16[128,4096]{1,0:T(8,128)(2,1)} fusion(bf16[1024,4096]{1,0:T(8,128)(2,1)} %gather_fusion.1, f32[128,8]{1,0:T(8,128)S(1)} %copy.10), kind=kLoop, calls=%fused_computation.3 | loop fusion | flops 12058624 | bytes 9441280 | tf_op jit(solution)/shard_map/reduce_sum | solution.py:42
  616.7 8.9 %fusion = f32[128,1,8]{2,1,0:T(1,128)S(1)} fusion(bf16[1024,4096]{1,0:T(8,128)(2,1)} %gather_fusion.1, bf16[128,4096,1]{1,0,2:T(8,128)(2,1)S(1)} %bitcast.40), kind=kOutput, calls=%fused_computation.5 | convolution fusion | flops 8388608 | bytes 9441280 | tf_op jit(solution)/shard_map/td,tkd->tk/dot_general | solution.py:45
  625.7 0.7 copy.17
  (21 shorter events, 0.4 us)
Async XLA Ops:
  0.6 2.9 copy-start
  261.4 12.3 %copy-start.2 = (bf16[1280,4096]{1,0:T(8,128)(2,1)S(1)}, bf16[1280,4096]{1,0:T(8,128)(2,1)}, u32[]{:S(2)}) copy-start(bf16[1280,4096]{1,0:T(8,128)(2,1)} %reshape.111) | copy-start | bytes 31457284
  313.6 13.1 %copy-start.3 = (f32[128,8]{0,1:T(8,128)S(1)}, f32[128,8]{0,1:T(8,128)}, u32[]{:S(2)}) copy-start(f32[128,8]{0,1:T(8,128)} %param.9) | copy-start | bytes 12292
  313.6 253.2 %all-to-all-start.1 = ((bf16[128,10,4096]{2,1,0:T(8,128)(2,1)}), bf16[128,10,4096]{2,1,0:T(8,128)(2,1)}, u32[]{:S(2)}, u32[]{:S(2)}) async-start(bf16[128,10,4096]{2,1,0:T(8,128)(2,1)} %reshape.112), calls=%async_computation.1 | async-start | bytes 33554432 | tf_op jit(solution)/shard_map/all_to_all | solution.py:38
  603.8 13.0 %copy-start.4 = (bf16[128,4096]{1,0:T(8,128)(2,1)S(1)}, bf16[128,4096]{1,0:T(8,128)(2,1)}, u32[]{:S(2)}) copy-start(bf16[128,4096]{1,0:T(8,128)(2,1)} %param.10) | copy-start | bytes 3145732
  616.7 9.6 %copy-start.1 = (bf16[128,4096]{1,0:T(8,128)(2,1)S(1)}, bf16[128,4096]{1,0:T(8,128)(2,1)}, u32[]{:S(2)}) copy-start(bf16[128,4096]{1,0:T(8,128)(2,1)} %param.7) | copy-start | bytes 3145732
where the time goes:
time: 635 us; the launch traced here: 627 us
  waiting for transfers between devices  240 us (38%)
  blocking collectives  199 us (31%)
  local copies, waits for them, and re-layouts  113 us (18%)
  matrix products  45.9 us (7%)
  other arithmetic  14.3 us (2%)
  starting transfers between devices  13.1 us (2%)
    all_to_all x1, waiting for transfers between devices, per_device(): lax.all_to_all(results, ('node', 'local'), split_axis=0, concat_axis=0, t...  240 us
    all_to_all x1, blocking collectives, per_device(): lax.all_to_all(outgoing, ('node', 'local'), split_axis=0, concat_axis=0,...  199 us
    gather x1, local copies, waits for them, and re-layouts, per_device(): returned.reshape(slot_total, model_width)[slot_ids]  20.4 us
    scatter x1, local copies, waits for them, and re-layouts, per_device(): jnp.zeros((slot_total, model_width), jnp.bfloat16).at[slot_ids]  19 us
    reshape x1, local copies, waits for them, and re-layouts, per_device(): received.reshape(slot_total, model_width)  16.5 us
    reshape x1, local copies, waits for them, and re-layouts, per_device(): returned.reshape(slot_total, model_width)[slot_ids]  16.5 us
    reshape x1, local copies, waits for them, and re-layouts, per_device(): outgoing = outgoing.reshape(expert_count, capacity, model_width)  15.2 us
    reshape x1, local copies, waits for them, and re-layouts, per_device(): results = results.reshape(expert_count, capacity, model_width)  15.2 us
  transfers between devices with their start and end apart: 1, of which 1 were waited for; matrix products, arithmetic and copies ran while one was open for 0% of the time, Pallas kernels for 0%

commit v1 on v0

v1 whole, which is shorter than its diff:
```python
import functools

import jax
import jax.numpy as jnp
from jax import lax
from jax.experimental import pallas as pl
from jax.experimental.pallas import tpu as pltpu
from jax.sharding import PartitionSpec as P

CAP = 10
QUARTERS = 4
MIB = 1 << 20


def iota(shape, dim):
    return lax.broadcasted_iota(jnp.int32, shape, dim)


def dot(a, b, dims=((1,), (0,))):
    return lax.dot_general(a, b, (dims, ((), ())), preferred_element_type=jnp.float32)


def to_quarters(rows):
    slots = rows // QUARTERS
    out, src = iota((rows, rows), 0), iota((rows, rows), 1)
    return (src == (out % slots) * QUARTERS + out // slots).astype(jnp.bfloat16)


def to_slots(rows):
    slots = rows // QUARTERS
    out, src = iota((rows, rows), 0), iota((rows, rows), 1)
    return (src == (out % QUARTERS) * slots + out // QUARTERS).astype(jnp.bfloat16)


def pack_kernel(experts, group, ids_ref, tokens_ref, out_ref, slot_ref, place, quartered):
    step = pl.program_id(0)
    tok = tokens_ref.shape[0]
    width = tokens_ref.shape[1] // QUARTERS

    @pl.when(step == 0)
    def _():
        ids = ids_ref[...]
        named = jnp.zeros((experts, tok), jnp.float32)
        for k in range(ids.shape[0]):
            named += (iota((experts, tok), 0) == ids[k : k + 1, :]).astype(jnp.float32)
        before = (iota((tok, tok), 0) < iota((tok, tok), 1)).astype(jnp.bfloat16)
        rank = dot(named.astype(jnp.bfloat16), before)
        place[...] = jnp.where(named > 0.5, rank, -1.0)
        slot_of = (rank + (iota((experts, tok), 0) * CAP).astype(jnp.float32)).astype(jnp.int32)
        for k in range(ids.shape[0]):
            chosen = iota((experts, tok), 0) == ids[k : k + 1, :]
            slot_ref[k : k + 1, :] = jnp.sum(jnp.where(chosen, slot_of, 0), axis=0, keepdims=True)
        for q in range(QUARTERS):
            quartered[q * tok : (q + 1) * tok, :] = tokens_ref[:, q * width : (q + 1) * width]

    rows = CAP * QUARTERS
    row, col = iota((rows, QUARTERS * tok), 0), iota((rows, QUARTERS * tok), 1)
    wanted = jnp.where(row % QUARTERS == col // tok, row // QUARTERS, -2).astype(jnp.float32)
    mine = place[pl.ds(pl.multiple_of(step * group, group), group), :]
    mine = jnp.concatenate([mine] * QUARTERS, axis=1)
    picks = [
        (mine[g : g + 1, :] == wanted).astype(jnp.float32).astype(jnp.bfloat16) for g in range(group)
    ]
    out_ref[...] = dot(jnp.concatenate(picks, axis=0), quartered[...]).astype(jnp.bfloat16)


def pack(ids_t, tokens, experts):
    tok, model = tokens.shape
    group = 16
    rows = CAP * QUARTERS
    width = model // QUARTERS
    return pl.pallas_call(
        functools.partial(pack_kernel, experts, group),
        grid=(experts // group,),
        in_specs=[
            pl.BlockSpec(ids_t.shape, lambda i: (0, 0)),
            pl.BlockSpec(tokens.shape, lambda i: (0, 0)),
        ],
        out_specs=[
            pl.BlockSpec((group * rows, width), lambda i: (i, 0)),
            pl.BlockSpec(ids_t.shape, lambda i: (0, 0)),
        ],
        out_shape=[
            jax.ShapeDtypeStruct((experts * rows, width), jnp.bfloat16),
            jax.ShapeDtypeStruct(ids_t.shape, jnp.int32),
        ],
        scratch_shapes=[
            pltpu.VMEM((experts, tok), jnp.float32),
            pltpu.VMEM((QUARTERS * tok, width), jnp.bfloat16),
        ],
        compiler_params=pltpu.CompilerParams(vmem_limit_bytes=40 * MIB),
    )(ids_t, tokens)


SUB = 256


def expert_kernel(x_ref, gate_hbm, up_hbm, down_hbm, y_ref, gate, up, down, xs, sems):
    step = pl.program_id(0)
    block = xs.shape[0]
    model, ff = gate.shape
    width = model // QUARTERS
    per = SUB // QUARTERS

    quarters = [pl.ds(q * width, width) for q in range(QUARTERS)]
    gates = [pltpu.make_async_copy(gate_hbm.at[p, :], gate.at[p, :], sems.at[0, q]) for q, p in enumerate(quarters)]
    ups = [pltpu.make_async_copy(up_hbm.at[p, :], up.at[p, :], sems.at[1, q]) for q, p in enumerate(quarters)]
    downs = pltpu.make_async_copy(down_hbm, down, sems.at[2, 0])

    def wait(*copies):
        @pl.when(step == 0)
        def _():
            for copy in copies:
                copy.wait()

    @pl.when(step == 0)
    def _():
        for q in range(QUARTERS):
            gates[q].start()
            ups[q].start()
        downs.start()

    order = to_quarters(SUB)
    for b in range(block // per):
        part = dot(order, x_ref[b * SUB : (b + 1) * SUB, :]).astype(jnp.bfloat16)
        for q in range(QUARTERS):
            xs[b * per : (b + 1) * per, q * width : (q + 1) * width] = part[q * per : (q + 1) * per, :]

    gate_act = jnp.zeros((block, ff), jnp.float32)
    up_act = jnp.zeros((block, ff), jnp.float32)
    for q in range(QUARTERS):
        part = slice(q * width, (q + 1) * width)
        wait(gates[q], ups[q])
        gate_act += dot(xs[:, part], gate[part, :])
        up_act += dot(xs[:, part], up[part, :])
    hidden = (gate_act / (1.0 + jnp.exp(-gate_act)) * up_act).astype(jnp.bfloat16)
    wait(downs)
    for q in range(QUARTERS):
        part = slice(q * width, (q + 1) * width)
        xs[:, part] = dot(hidden, down[:, part]).astype(jnp.bfloat16)
    back = to_slots(SUB)
    for b in range(block // per):
        part = jnp.concatenate(
            [xs[b * per : (b + 1) * per, q * width : (q + 1) * width] for q in range(QUARTERS)], axis=0
        )
        y_ref[b * SUB : (b + 1) * SUB, :] = dot(back, part).astype(jnp.bfloat16)


def expert_apply(x, gate, up, down, block=256):
    model, ff = gate.shape
    width = model // QUARTERS
    rows = x.shape[0]
    return pl.pallas_call(
        expert_kernel,
        grid=(rows // (block * QUARTERS),),
        in_specs=[pl.BlockSpec((block * QUARTERS, width), lambda i: (i, 0))]
        + [pl.BlockSpec(memory_space=pl.ANY)] * 3,
        out_specs=pl.BlockSpec((block * QUARTERS, width), lambda i: (i, 0)),
        out_shape=jax.ShapeDtypeStruct(x.shape, jnp.bfloat16),
        scratch_shapes=[
            pltpu.VMEM(gate.shape, jnp.bfloat16),
            pltpu.VMEM(up.shape, jnp.bfloat16),
            pltpu.VMEM(down.shape, jnp.bfloat16),
            pltpu.VMEM((block, model), jnp.bfloat16),
            pltpu.SemaphoreType.DMA((3, QUARTERS)),
        ],
        compiler_params=pltpu.CompilerParams(vmem_limit_bytes=60 * MIB),
    )(x, gate, up, down)


def combine_kernel(slot_ref, probs_ref, cot_ref, y_ref, mixed_ref, grads_ref, xs):
    slots = xs.shape[0]
    tok, model = cot_ref.shape
    width = model // QUARTERS
    per = SUB // QUARTERS
    order = to_quarters(SUB)
    for b in range(slots // per):
        part = dot(order, y_ref[b * SUB : (b + 1) * SUB, :]).astype(jnp.bfloat16)
        for q in range(QUARTERS):
            xs[b * per : (b + 1) * per, q * width : (q + 1) * width] = part[q * per : (q + 1) * per, :]
    inner = dot(xs[...], cot_ref[...], ((1,), (1,)))
    here = iota((slots, tok), 0)
    weight = jnp.zeros((slots, tok), jnp.float32)
    for k in range(slot_ref.shape[0]):
        mask = here == slot_ref[k : k + 1, :]
        weight += jnp.where(mask, probs_ref[k : k + 1, :], 0.0)
        grads_ref[k : k + 1, :] = jnp.sum(jnp.where(mask, inner, 0.0), axis=0, keepdims=True)
    weight = weight.T
    high = weight.astype(jnp.bfloat16)
    low = (weight - high.astype(jnp.float32)).astype(jnp.bfloat16)
    both = jnp.concatenate([high, low], axis=0)
    for q in range(QUARTERS):
        part = slice(q * width, (q + 1) * width)
        total = dot(both, xs[:, part])
        mixed_ref[:, part] = (total[:tok] + total[tok:]).astype(jnp.bfloat16)


def combine(slot_t, probs_t, cotangent, y):
    model = cotangent.shape[1]
    return pl.pallas_call(
        combine_kernel,
        out_shape=[
            jax.ShapeDtypeStruct(cotangent.shape, jnp.bfloat16),
            jax.ShapeDtypeStruct(probs_t.shape, jnp.float32),
        ],
        scratch_shapes=[pltpu.VMEM((y.shape[0] // QUARTERS, model), jnp.bfloat16)],
        compiler_params=pltpu.CompilerParams(vmem_limit_bytes=40 * MIB),
    )(slot_t, probs_t, cotangent, y)


def exchange(rows, devices):
    parts = rows.reshape(devices, rows.shape[0] // devices, rows.shape[1])
    parts = lax.all_to_all(parts, ("node", "local"), split_axis=0, concat_axis=0, tiled=True)
    return parts.reshape(rows.shape)


def per_device(tokens, expert_ids, route_probs, cotangent, gate_weight, up_weight, down_weight):
    devices = lax.axis_size("node") * lax.axis_size("local")
    packed, slot_t = pack(expert_ids.T, tokens, devices)
    received = exchange(packed, devices)
    results = expert_apply(received, gate_weight[0], up_weight[0], down_weight[0])
    returned = exchange(results, devices)
    mixed, grads_t = combine(slot_t, route_probs.T, cotangent, returned)
    return mixed, grads_t.T


def solution(mesh):
    placed = (P(("node", "local"), None),) * 4 + (P(("node", "local"), None, None),) * 3
    return jax.shard_map(
        per_device,
        mesh=mesh,
        in_specs=placed,
        out_specs=(P(("node", "local"), None), P(("node", "local"), None)),
        check_vma=False,
    )
```

time: 635 us -> 321 us (0.51)
  waiting for transfers between devices: 240 us -> 0 us
  local copies, waits for them, and re-layouts: 113 us -> 1.92 us
  blocking collectives: 199 us -> 257 us
  Pallas kernels: 0 us -> 56.5 us
  matrix products: 45.9 us -> 0 us
  other arithmetic: 14.3 us -> 0 us
  starting transfers between devices: 13.1 us -> 0 us
    all_to_all x1 -> x0, waiting for transfers between devices: 240 us -> none  [per_device(): lax.all_to_all(results, ('node', 'local'), split_axis=0, concat_axis=0, t...]
    reshape x4 -> x0, local copies, waits for them, and re-layouts: 63.4 us -> none  [the longest x1 16.5 us: per_device(): received.reshape(slot_total, model_width)]
    all_to_all x1 -> x2, blocking collectives: 199 us -> 257 us  [exchange(): lax.all_to_all(parts, ('node', 'local'), split_axis=0, concat_axis=0, til...]
    pallas_call x0 -> x3, Pallas kernels: none -> 56.5 us  [the longest x1 39.3 us: expert_apply(): pl.pallas_call(expert_kernel, grid=(rows // (block * QUARTERS),), in_spec...]
    dot_general x4 -> x0, matrix products: 45.9 us -> none  [the longest x1 13.5 us: expert_apply(): jnp.dot(hidden, down_mat, preferred_element_type=jnp.float32)]
    gather x2 -> x0, local copies, waits for them, and re-layouts: 28.1 us -> none  [the longest x1 20.4 us: per_device(): returned.reshape(slot_total, model_width)[slot_ids]]
    scatter x1 -> x0, local copies, waits for them, and re-layouts: 19 us -> none  [per_device(): jnp.zeros((slot_total, model_width), jnp.bfloat16).at[slot_ids]]
    reduce_sum x2 -> x0, other arithmetic: 13.3 us -> none  [the longest x1 13 us: per_device(): jnp.sum(route_probs[:, :, None] * pair_out.astype(jnp.float32), axis=1)]
  transfers between devices with their start and end apart: 1 -> 0, of which waited for: 1 -> 0; matrix products, arithmetic and copies ran while one was open for 0% -> 0% of each run, Pallas kernels for 0% -> 0%
where the time goes in v1:
time: 321 us; the launch traced here: 316 us
  blocking collectives  257 us (80%)
  Pallas kernels  56.5 us (18%)
    all_to_all x2, blocking collectives, exchange(): lax.all_to_all(parts, ('node', 'local'), split_axis=0, concat_axis=0, til...  257 us
    pallas_call x1, Pallas kernels, expert_apply(): pl.pallas_call(expert_kernel, grid=(rows // (block * QUARTERS),), in_spec...  39.3 us
    pallas_call x1, Pallas kernels, combine(): pl.pallas_call(combine_kernel, out_shape=[jax.ShapeDtypeStruct(cotangent....  10.1 us
    pallas_call x1, Pallas kernels, pack(): pl.pallas_call(functools.partial(pack_kernel, experts, group), grid=(expe...  7.05 us

profile of v1, /device:TPU:66, one launch (start us, length us, event | category | flops | bytes accessed | tf_op | source)
XLA Modules:
  0.0 315.6 jit_solution(1605040713245699465)
XLA Ops:
  0.6 0.0 copy-start.1
  0.6 1.2 copy-done.1
  1.9 0.0 copy-start.3
  1.9 0.7 copy-done.3
  2.5 7.0 %shard_map.86 = (bf16[5120,1024]{1,0:T(8,128)(2,1)S(1)}, s32[8,128]{1,0:T(8,128)S(1)}) custom-call(s32[8,128]{1,0:T(8,128)S(1)} %bitcast.13, bf16[128,4096]{1,0:T(8,128)(2,1)S(1)} %copy-done.1), custom_call_target="tpu_custom_call" | custom-call | tf_op jit(solution)/shard_map/pallas_call | solution.py:72
  9.6 128.1 %all_to_all.10 = bf16[128,40,1024]{2,1,0:T(8,128)(2,1)} all-to-all(bf16[128,40,1024]{2,1,0:T(8,128)(2,1)S(1)} %bitcast.11), channel_id=1, replica_groups=mesh['node'=16,'local'=8] {'node','local'}, dimensions={0} | all-to-all | bytes 20971520 | tf_op jit(solution)/shard_map/all_to_all | solution.py:213
  137.7 39.3 %shard_map.87 = bf16[5120,1024]{1,0:T(8,128)(2,1)} custom-call(bf16[5120,1024]{1,0:T(8,128)(2,1)} %bitcast.14, bf16[4096,768]{1,0:T(8,128)(2,1)} %bitcast.16, bf16[4096,768]{1,0:T(8,128)(2,1)} %bitcast.17, bf16[768,4096]{1,0:T(8,128)(2,1)} %bitcast.18), custom_call_target="tpu_custom_call" | custom-call | tf_op jit(solution)/shard_map/pallas_call | solution.py:153
  176.9 0.0 copy-start
  176.9 0.0 copy-start.2
  177.0 128.5 %all_to_all.11 = bf16[128,40,1024]{2,1,0:T(8,128)(2,1)S(1)} all-to-all(bf16[128,40,1024]{2,1,0:T(8,128)(2,1)} %bitcast.15), channel_id=1, replica_groups=mesh['node'=16,'local'=8] {'node','local'}, dimensions={0} | all-to-all | bytes 20971520 | tf_op jit(solution)/shard_map/all_to_all | solution.py:213
  305.4 0.0 copy-done
  305.4 0.0 copy-done.2
  305.4 10.1 %shard_map.88 = (bf16[128,4096]{1,0:T(8,128)(2,1)}, f32[8,128]{1,0:T(8,128)}) custom-call(s32[8,128]{1,0:T(8,128)S(1)} %get-tuple-element.6.slot_ref, f32[8,128]{1,0:T(8,128)S(1)} %bitcast.12, bf16[128,4096]{1,0:T(8,128)(2,1)S(1)} %copy-done, bf16[5120,1024]{1,0:T(8,128)(2,1)S(1)} %bitcast.10), custom_call_target="tpu_custom_call" | custom-call | tf_op jit(solution)/shard_map/pallas_call | solution.py:200
Async XLA Ops:
  0.6 1.2 copy-start.1
  1.9 0.7 copy-start.3
  176.9 128.5 %copy-start = (bf16[128,4096]{1,0:T(8,128)(2,1)S(1)}, bf16[128,4096]{1,0:T(8,128)(2,1)}, u32[]{:S(2)}) copy-start(bf16[128,4096]{1,0:T(8,128)(2,1)} %cot_ref.1) | copy-start | bytes 3145732
  176.9 128.5 %copy-start.2 = (f32[128,8]{0,1:T(8,128)S(1)}, f32[128,8]{0,1:T(8,128)}, u32[]{:S(2)}) copy-start(f32[128,8]{0,1:T(8,128)} %param.9) | copy-start | bytes 12292

commit v2 on v1

--- a/solution.py
+++ b/solution.py
@@ -9,6 +9,9 @@
 
 CAP = 10
 QUARTERS = 4
+MAIN = 8
+TAIL = CAP - MAIN
+ROWS = CAP * QUARTERS
 MIB = 1 << 20
 
 
@@ -32,6 +35,28 @@
     return (src == (out % QUARTERS) * slots + out // QUARTERS).astype(jnp.bfloat16)
 
 
+def unpack(messages, x_ref, xs, tails):
+    width = x_ref.shape[1]
+    for pair in range(messages // 2):
+        both = x_ref[pair * 2 * ROWS : (pair + 1) * 2 * ROWS, :].astype(jnp.float32)
+        for q in range(QUARTERS + 1):
+            first = both[q * MAIN : (q + 1) * MAIN, :]
+            second = both[ROWS + q * MAIN : ROWS + (q + 1) * MAIN, :]
+            rows = jnp.concatenate([first, second], axis=0).astype(jnp.bfloat16)
+            if q < QUARTERS:
+                xs[pair * 2 * MAIN : (pair + 1) * 2 * MAIN, q * width : (q + 1) * width] = rows
+            else:
+                tails[pair * 2 * MAIN : (pair + 1) * 2 * MAIN, :] = rows
+    sub = 32 * MAIN
+    per = sub // QUARTERS
+    order = to_quarters(sub)
+    for b in range(messages // 32):
+        part = dot(order, tails[b * sub : (b + 1) * sub, :]).astype(jnp.bfloat16)
+        base = messages * MAIN + b * per
+        for q in range(QUARTERS):
+            xs[base : base + per, q * width : (q + 1) * width] = part[q * per : (q + 1) * per, :]
+
+
 def pack_kernel(experts, group, ids_ref, tokens_ref, out_ref, slot_ref, place, quartered):
     step = pl.program_id(0)
     tok = tokens_ref.shape[0]
@@ -40,34 +65,40 @@
     @pl.when(step == 0)
     def _():
         ids = ids_ref[...]
+        expert = iota((experts, tok), 0)
         named = jnp.zeros((experts, tok), jnp.float32)
         for k in range(ids.shape[0]):
-            named += (iota((experts, tok), 0) == ids[k : k + 1, :]).astype(jnp.float32)
+            named += (expert == ids[k : k + 1, :]).astype(jnp.float32)
         before = (iota((tok, tok), 0) < iota((tok, tok), 1)).astype(jnp.bfloat16)
         rank = dot(named.astype(jnp.bfloat16), before)
         place[...] = jnp.where(named > 0.5, rank, -1.0)
-        slot_of = (rank + (iota((experts, tok), 0) * CAP).astype(jnp.float32)).astype(jnp.int32)
+        rank = rank.astype(jnp.int32)
+        slot_of = jnp.where(rank < MAIN, expert * MAIN + rank, experts * MAIN + expert * TAIL + rank - MAIN)
         for k in range(ids.shape[0]):
-            chosen = iota((experts, tok), 0) == ids[k : k + 1, :]
+            chosen = expert == ids[k : k + 1, :]
             slot_ref[k : k + 1, :] = jnp.sum(jnp.where(chosen, slot_of, 0), axis=0, keepdims=True)
         for q in range(QUARTERS):
             quartered[q * tok : (q + 1) * tok, :] = tokens_ref[:, q * width : (q + 1) * width]
 
-    rows = CAP * QUARTERS
-    row, col = iota((rows, QUARTERS * tok), 0), iota((rows, QUARTERS * tok), 1)
-    wanted = jnp.where(row % QUARTERS == col // tok, row // QUARTERS, -2).astype(jnp.float32)
     mine = place[pl.ds(pl.multiple_of(step * group, group), group), :]
-    mine = jnp.concatenate([mine] * QUARTERS, axis=1)
-    picks = [
-        (mine[g : g + 1, :] == wanted).astype(jnp.float32).astype(jnp.bfloat16) for g in range(group)
-    ]
-    out_ref[...] = dot(jnp.concatenate(picks, axis=0), quartered[...]).astype(jnp.bfloat16)
+    wide = jnp.concatenate([mine] * QUARTERS, axis=1)
+    rank = iota((MAIN, tok), 0).astype(jnp.float32)
+    row, col = iota((MAIN, QUARTERS * tok), 0), iota((MAIN, QUARTERS * tok), 1)
+    late = jnp.where(row % QUARTERS == col // tok, MAIN + row // QUARTERS, -2).astype(jnp.float32)
+    main = [(mine[g : g + 1, :] == rank).astype(jnp.float32) for g in range(group)]
+    tail = [(wide[g : g + 1, :] == late).astype(jnp.float32) for g in range(group)]
+    main = jnp.concatenate(main, axis=0).astype(jnp.bfloat16)
+    tail = jnp.concatenate(tail, axis=0).astype(jnp.bfloat16)
+    parts = [dot(main, quartered[q * tok : (q + 1) * tok, :]) for q in range(QUARTERS)]
+    parts.append(dot(tail, quartered[...]))
+    for pair in range(group // 2):
+        both = [p[(2 * pair + g) * MAIN : (2 * pair + g + 1) * MAIN, :] for g in range(2) for p in parts]
+        out_ref[pair * 2 * ROWS : (pair + 1) * 2 * ROWS, :] = jnp.concatenate(both, axis=0).astype(jnp.bfloat16)
 
 
 def pack(ids_t, tokens, experts):
     tok, model = tokens.shape
-    group = 16
-    rows = CAP * QUARTERS
+    group = 32
     width = model // QUARTERS
     return pl.pallas_call(
         functools.partial(pack_kernel, experts, group),
@@ -77,11 +108,11 @@
             pl.BlockSpec(tokens.shape, lambda i: (0, 0)),
         ],
         out_specs=[
-            pl.BlockSpec((group * rows, width), lambda i: (i, 0)),
+            pl.BlockSpec((group * ROWS, width), lambda i: (i, 0)),
             pl.BlockSpec(ids_t.shape, lambda i: (0, 0)),
         ],
         out_shape=[
-            jax.ShapeDtypeStruct((experts * rows, width), jnp.bfloat16),
+            jax.ShapeDtypeStruct((experts * ROWS, width), jnp.bfloat16),
             jax.ShapeDtypeStruct(ids_t.shape, jnp.int32),
         ],
         scratch_shapes=[
@@ -92,15 +123,12 @@
     )(ids_t, tokens)
 
 
-SUB = 256
-
-
-def expert_kernel(x_ref, gate_hbm, up_hbm, down_hbm, y_ref, gate, up, down, xs, sems):
+def expert_kernel(x_ref, gate_hbm, up_hbm, down_hbm, y_ref, gate, up, down, xs, ys, tails, sems):
     step = pl.program_id(0)
     block = xs.shape[0]
+    messages = block // CAP
     model, ff = gate.shape
     width = model // QUARTERS
-    per = SUB // QUARTERS
 
     quarters = [pl.ds(q * width, width) for q in range(QUARTERS)]
     gates = [pltpu.make_async_copy(gate_hbm.at[p, :], gate.at[p, :], sems.at[0, q]) for q, p in enumerate(quarters)]
@@ -120,12 +148,7 @@
             ups[q].start()
         downs.start()
 
-    order = to_quarters(SUB)
-    for b in range(block // per):
-        part = dot(order, x_ref[b * SUB : (b + 1) * SUB, :]).astype(jnp.bfloat16)
-        for q in range(QUARTERS):
-            xs[b * per : (b + 1) * per, q * width : (q + 1) * width] = part[q * per : (q + 1) * per, :]
-
+    unpack(messages, x_ref, xs, tails)
     gate_act = jnp.zeros((block, ff), jnp.float32)
     up_act = jnp.zeros((block, ff), jnp.float32)
     for q in range(QUARTERS):
@@ -137,47 +160,47 @@
     wait(downs)
     for q in range(QUARTERS):
         part = slice(q * width, (q + 1) * width)
-        xs[:, part] = dot(hidden, down[:, part]).astype(jnp.bfloat16)
-    back = to_slots(SUB)
-    for b in range(block // per):
-        part = jnp.concatenate(
-            [xs[b * per : (b + 1) * per, q * width : (q + 1) * width] for q in range(QUARTERS)], axis=0
-        )
-        y_ref[b * SUB : (b + 1) * SUB, :] = dot(back, part).astype(jnp.bfloat16)
-
-
-def expert_apply(x, gate, up, down, block=256):
+        ys[:, part] = dot(hidden, down[:, part])
+    main = messages * MAIN
+    late = [ys[main:, q * width : (q + 1) * width].astype(jnp.bfloat16) for q in range(QUARTERS)]
+    late = dot(to_slots(messages * MAIN), jnp.concatenate(late, axis=0))
+    for pair in range(messages // 2):
+        both = []
+        for m in (2 * pair, 2 * pair + 1):
+            both += [ys[m * MAIN : (m + 1) * MAIN, q * width : (q + 1) * width] for q in range(QUARTERS)]
+            both.append(late[m * MAIN : (m + 1) * MAIN, :])
+        y_ref[pair * 2 * ROWS : (pair + 1) * 2 * ROWS, :] = jnp.concatenate(both, axis=0).astype(jnp.bfloat16)
+
+
+def expert_apply(x, gate, up, down, messages=32):
     model, ff = gate.shape
     width = model // QUARTERS
-    rows = x.shape[0]
+    block = messages * CAP
     return pl.pallas_call(
         expert_kernel,
-        grid=(rows // (block * QUARTERS),),
-        in_specs=[pl.BlockSpec((block * QUARTERS, width), lambda i: (i, 0))]
+        grid=(x.shape[0] // (messages * ROWS),),
+        in_specs=[pl.BlockSpec((messages * ROWS, width), lambda i: (i, 0))]
         + [pl.BlockSpec(memory_space=pl.ANY)] * 3,
-        out_specs=pl.BlockSpec((block * QUARTERS, width), lambda i: (i, 0)),
+        out_specs=pl.BlockSpec((messages * ROWS, width), lambda i: (i, 0)),
         out_shape=jax.ShapeDtypeStruct(x.shape, jnp.bfloat16),
         scratch_shapes=[
             pltpu.VMEM(gate.shape, jnp.bfloat16),
             pltpu.VMEM(up.shape, jnp.bfloat16),
             pltpu.VMEM(down.shape, jnp.bfloat16),
             pltpu.VMEM((block, model), jnp.bfloat16),
+            pltpu.VMEM((block, model), jnp.float32),
+            pltpu.VMEM((messages * MAIN, width), jnp.bfloat16),
             pltpu.SemaphoreType.DMA((3, QUARTERS)),
         ],
         compiler_params=pltpu.CompilerParams(vmem_limit_bytes=60 * MIB),
     )(x, gate, up, down)
 
 
-def combine_kernel(slot_ref, probs_ref, cot_ref, y_ref, mixed_ref, grads_ref, xs):
+def combine_kernel(slot_ref, probs_ref, cot_ref, y_ref, mixed_ref, grads_ref, xs, tails):
     slots = xs.shape[0]
     tok, model = cot_ref.shape
     width = model // QUARTERS
-    per = SUB // QUARTERS
-    order = to_quarters(SUB)
-    for b in range(slots // per):
-        part = dot(order, y_ref[b * SUB : (b + 1) * SUB, :]).astype(jnp.bfloat16)
-        for q in range(QUARTERS):
-            xs[b * per : (b + 1) * per, q * width : (q + 1) * width] = part[q * per : (q + 1) * per, :]
+    unpack(slots // CAP, y_ref, xs, tails)
     inner = dot(xs[...], cot_ref[...], ((1,), (1,)))
     here = iota((slots, tok), 0)
     weight = jnp.zeros((slots, tok), jnp.float32)
@@ -197,13 +220,17 @@
 
 def combine(slot_t, probs_t, cotangent, y):
     model = cotangent.shape[1]
+    slots = y.shape[0] // QUARTERS
     return pl.pallas_call(
         combine_kernel,
         out_shape=[
             jax.ShapeDtypeStruct(cotangent.shape, jnp.bfloat16),
             jax.ShapeDtypeStruct(probs_t.shape, jnp.float32),
         ],
-        scratch_shapes=[pltpu.VMEM((y.shape[0] // QUARTERS, model), jnp.bfloat16)],
+        scratch_shapes=[
+            pltpu.VMEM((slots, model), jnp.bfloat16),
+            pltpu.VMEM((slots // CAP * MAIN, y.shape[1]), jnp.bfloat16),
+        ],
         compiler_params=pltpu.CompilerParams(vmem_limit_bytes=40 * MIB),
     )(slot_t, probs_t, cotangent, y)
 

time: 321 us -> 312 us (0.972)
  Pallas kernels: 56.5 us -> 47.5 us
    pallas_call x1, Pallas kernels: 39.3 us -> 35.3 us  [expert_apply(): pl.pallas_call(expert_kernel, grid=(x.shape[0] // (messages * ROWS),), in...]
where the time goes in v2:
time: 312 us; the launch traced here: 307 us
  blocking collectives  257 us (82%)
  Pallas kernels  47.5 us (15%)
    all_to_all x2, blocking collectives, exchange(): lax.all_to_all(parts, ('node', 'local'), split_axis=0, concat_axis=0, til...  257 us
    pallas_call x1, Pallas kernels, expert_apply(): pl.pallas_call(expert_kernel, grid=(x.shape[0] // (messages * ROWS),), in...  35.3 us
    pallas_call x1, Pallas kernels, combine(): pl.pallas_call(combine_kernel, out_shape=[jax.ShapeDtypeStruct(cotangent....  8.01 us

profile of v2, /device:TPU:66, one launch (start us, length us, event | category | flops | bytes accessed | tf_op | source)
XLA Modules:
  0.0 306.6 jit_solution(4317278232601020434)
XLA Ops:
  0.6 0.0 copy-start.1
  0.6 1.2 copy-done.1
  1.9 0.0 copy-start.3
  1.9 0.7 copy-done.3
  2.5 4.2 %shard_map.86 = (bf16[5120,1024]{1,0:T(8,128)(2,1)S(1)}, s32[8,128]{1,0:T(8,128)S(1)}) custom-call(s32[8,128]{1,0:T(8,128)S(1)} %bitcast.13, bf16[128,4096]{1,0:T(8,128)(2,1)S(1)} %copy-done.1), custom_call_target="tpu_custom_call" | custom-call | tf_op jit(solution)/shard_map/pallas_call | solution.py:103
  6.7 128.1 %all_to_all.10 = bf16[128,40,1024]{2,1,0:T(8,128)(2,1)} all-to-all(bf16[128,40,1024]{2,1,0:T(8,128)(2,1)S(1)} %bitcast.11), channel_id=1, replica_groups=mesh['node'=16,'local'=8] {'node','local'}, dimensions={0} | all-to-all | bytes 20971520 | tf_op jit(solution)/shard_map/all_to_all | solution.py:240
  134.8 35.3 %shard_map.87 = bf16[5120,1024]{1,0:T(8,128)(2,1)} custom-call(bf16[5120,1024]{1,0:T(8,128)(2,1)} %bitcast.14, bf16[4096,768]{1,0:T(8,128)(2,1)} %bitcast.16, bf16[4096,768]{1,0:T(8,128)(2,1)} %bitcast.17, bf16[768,4096]{1,0:T(8,128)(2,1)} %bitcast.18), custom_call_target="tpu_custom_call" | custom-call | tf_op jit(solution)/shard_map/pallas_call | solution.py:179
  170.1 0.0 copy-start
  170.1 0.0 copy-start.2
  170.1 128.4 %all_to_all.11 = bf16[128,40,1024]{2,1,0:T(8,128)(2,1)S(1)} all-to-all(bf16[128,40,1024]{2,1,0:T(8,128)(2,1)} %bitcast.15), channel_id=1, replica_groups=mesh['node'=16,'local'=8] {'node','local'}, dimensions={0} | all-to-all | bytes 20971520 | tf_op jit(solution)/shard_map/all_to_all | solution.py:240
  298.6 0.0 copy-done
  298.6 0.0 copy-done.2
  298.6 8.0 %shard_map.88 = (bf16[128,4096]{1,0:T(8,128)(2,1)}, f32[8,128]{1,0:T(8,128)}) custom-call(s32[8,128]{1,0:T(8,128)S(1)} %get-tuple-element.6.slot_ref, f32[8,128]{1,0:T(8,128)S(1)} %bitcast.12, bf16[128,4096]{1,0:T(8,128)(2,1)S(1)} %copy-done, bf16[5120,1024]{1,0:T(8,128)(2,1)S(1)} %bitcast.10), custom_call_target="tpu_custom_call" | custom-call | tf_op jit(solution)/shard_map/pallas_call | solution.py:224
Async XLA Ops:
  0.6 1.2 copy-start.1
  1.9 0.7 copy-start.3
  170.1 128.5 %copy-start = (bf16[128,4096]{1,0:T(8,128)(2,1)S(1)}, bf16[128,4096]{1,0:T(8,128)(2,1)}, u32[]{:S(2)}) copy-start(bf16[128,4096]{1,0:T(8,128)(2,1)} %cot_ref.1) | copy-start | bytes 3145732
  170.1 128.5 %copy-start.2 = (f32[128,8]{0,1:T(8,128)S(1)}, f32[128,8]{0,1:T(8,128)}, u32[]{:S(2)}) copy-start(f32[128,8]{0,1:T(8,128)} %param.9) | copy-start | bytes 12292

commit v3 on v1

v3 whole, which is shorter than its diff:
```python
import functools

import jax
import jax.numpy as jnp
from jax import lax
from jax.experimental import pallas as pl
from jax.experimental.pallas import tpu as pltpu
from jax.sharding import PartitionSpec as P

CAP = 10
PARTS = 8
MAIN = 8
TAIL = CAP - MAIN
TILE = 2 * MAIN
BODY = PARTS * MAIN
ROWS = CAP * PARTS
SUB = 256
MIB = 1 << 20


def iota(shape, dim):
    return lax.broadcasted_iota(jnp.int32, shape, dim)


def dot(a, b, dims=((1,), (0,))):
    return lax.dot_general(a, b, (dims, ((), ())), preferred_element_type=jnp.float32)


def tails_in(x_ref, xs, base):
    width = x_ref.shape[2]
    slots = SUB // PARTS
    out, src = iota((SUB, SUB), 0), iota((SUB, SUB), 1)
    order = (src == (out % slots) * PARTS + out // slots).astype(jnp.bfloat16)
    per = SUB // TILE
    for b in range(x_ref.shape[0] // per):
        rows = x_ref[b * per : (b + 1) * per, BODY:ROWS, :].reshape(SUB, width)
        rows = dot(order, rows).astype(jnp.bfloat16)
        for q in range(PARTS):
            xs[base + b * slots : base + (b + 1) * slots, q * width : (q + 1) * width] = rows[q * slots : (q + 1) * slots, :]


def tails_out(tails, out_ref):
    width = out_ref.shape[2]
    slots = SUB // PARTS
    out, src = iota((SUB, SUB), 0), iota((SUB, SUB), 1)
    order = (src == (out % PARTS) * slots + out // PARTS).astype(jnp.bfloat16)
    per = SUB // TILE
    for b in range(out_ref.shape[0] // per):
        rows = [tails[b * slots : (b + 1) * slots, q * width : (q + 1) * width] for q in range(PARTS)]
        rows = dot(order, jnp.concatenate(rows, axis=0)).astype(jnp.bfloat16)
        out_ref[b * per : (b + 1) * per, BODY:ROWS, :] = rows.reshape(per, TILE, width)


def main_in(x_ref, xs, j, step=32):
    width = x_ref.shape[2]
    for b in range(0, x_ref.shape[0], step):
        both = x_ref[b : b + step, j * TILE : (j + 1) * TILE, :].astype(jnp.float32)
        for half in range(2):
            rows = both[:, half * MAIN : (half + 1) * MAIN, :].reshape(step * MAIN, width)
            q = 2 * j + half
            xs[b * MAIN : (b + step) * MAIN, q * width : (q + 1) * width] = rows.astype(jnp.bfloat16)


def main_out(rows, out_ref, j):
    messages, _, width = out_ref.shape
    halves = [rows[:, h * width : (h + 1) * width].reshape(messages, MAIN, width) for h in range(2)]
    out_ref[:, j * TILE : (j + 1) * TILE, :] = jnp.concatenate(halves, axis=1).astype(jnp.bfloat16)


def pack_kernel(experts, ids_ref, tokens_ref, out_ref, slot_ref, place, tails):
    step = pl.program_id(0)
    tok, model = tokens_ref.shape
    group = out_ref.shape[0]
    span = model // PARTS * 2

    @pl.when(step == 0)
    def _():
        ids = ids_ref[...]
        expert = iota((experts, tok), 0)
        named = jnp.zeros((experts, tok), jnp.float32)
        for k in range(ids.shape[0]):
            named += (expert == ids[k : k + 1, :]).astype(jnp.float32)
        before = (iota((tok, tok), 0) < iota((tok, tok), 1)).astype(jnp.bfloat16)
        rank = dot(named.astype(jnp.bfloat16), before)
        place[...] = jnp.where(named > 0.5, rank, -1.0)
        rank = rank.astype(jnp.int32)
        slot_of = jnp.where(rank < MAIN, expert * MAIN + rank, experts * MAIN + expert * TAIL + rank - MAIN)
        for k in range(ids.shape[0]):
            chosen = expert == ids[k : k + 1, :]
            slot_ref[k : k + 1, :] = jnp.sum(jnp.where(chosen, slot_of, 0), axis=0, keepdims=True)

    mine = place[pl.ds(pl.multiple_of(step * group, group), group), :]
    rank = iota((MAIN, tok), 0).astype(jnp.float32)
    main = [(mine[g : g + 1, :] == rank).astype(jnp.float32) for g in range(group)]
    main = jnp.concatenate(main, axis=0).astype(jnp.bfloat16)
    row = iota((MAIN, tok), 0)
    late = []
    for g in range(0, group, MAIN // TAIL):
        match = jnp.zeros((MAIN, tok), jnp.float32)
        for h in range(MAIN // TAIL):
            rank = jnp.where(row // TAIL == h, MAIN + row % TAIL, -2).astype(jnp.float32)
            match += (mine[g + h : g + h + 1, :] == rank).astype(jnp.float32)
        late.append(match)
    late = jnp.concatenate(late, axis=0).astype(jnp.bfloat16)
    for j in range(PARTS // 2):
        part = slice(j * span, (j + 1) * span)
        tails[:, part] = dot(late, tokens_ref[:, part]).astype(jnp.bfloat16)
        main_out(dot(main, tokens_ref[:, part]), out_ref, j)
    tails_out(tails, out_ref)


def pack(ids_t, tokens, experts):
    tok, model = tokens.shape
    group = 32
    shape = (ROWS, model // PARTS)
    return pl.pallas_call(
        functools.partial(pack_kernel, experts),
        grid=(experts // group,),
        in_specs=[
            pl.BlockSpec(ids_t.shape, lambda i: (0, 0)),
            pl.BlockSpec(tokens.shape, lambda i: (0, 0)),
        ],
        out_specs=[
            pl.BlockSpec((group, *shape), lambda i: (i, 0, 0)),
            pl.BlockSpec(ids_t.shape, lambda i: (0, 0)),
        ],
        out_shape=[
            jax.ShapeDtypeStruct((experts, *shape), jnp.bfloat16),
            jax.ShapeDtypeStruct(ids_t.shape, jnp.int32),
        ],
        scratch_shapes=[
            pltpu.VMEM((experts, tok), jnp.float32),
            pltpu.VMEM((group * TAIL, model), jnp.bfloat16),
        ],
        compiler_params=pltpu.CompilerParams(vmem_limit_bytes=14 * MIB),
    )(ids_t, tokens)


def expert_kernel(x_ref, gate, up, down, y_ref, xs, tails):
    main = x_ref.shape[0] * MAIN
    model = gate.shape[0]
    span = model // PARTS * 2
    tails_in(x_ref, xs, main)
    gate_act, up_act = 0.0, 0.0
    for j in range(PARTS // 2):
        part = slice(j * span, (j + 1) * span)
        main_in(x_ref, xs, j)
        gate_act += dot(xs[:, part], gate[part, :])
        up_act += dot(xs[:, part], up[part, :])
    hidden = (gate_act / (1.0 + jnp.exp(-gate_act)) * up_act).astype(jnp.bfloat16)
    for j in range(PARTS // 2):
        part = slice(j * span, (j + 1) * span)
        result = dot(hidden, down[:, part])
        main_out(result[:main], y_ref, j)
        tails[:, part] = result[main:].astype(jnp.bfloat16)
    tails_out(tails, y_ref)


def expert_apply(x, gate, up, down, messages=32):
    model = gate.shape[0]
    block = pl.BlockSpec((messages, *x.shape[1:]), lambda i: (i, 0, 0))
    return pl.pallas_call(
        expert_kernel,
        grid=(x.shape[0] // messages,),
        in_specs=[block] + [pl.BlockSpec(memory_space=pltpu.VMEM)] * 3,
        out_specs=block,
        out_shape=jax.ShapeDtypeStruct(x.shape, jnp.bfloat16),
        scratch_shapes=[
            pltpu.VMEM((messages * CAP, model), jnp.bfloat16),
            pltpu.VMEM((messages * TAIL, model), jnp.bfloat16),
        ],
        compiler_params=pltpu.CompilerParams(vmem_limit_bytes=24 * MIB),
    )(x, gate, up, down)


def combine_kernel(slot_ref, probs_ref, cot_ref, y_ref, mixed_ref, grads_ref, xs):
    slots, model = xs.shape
    tok = cot_ref.shape[0]
    span = model // PARTS * 2
    here = iota((slots, tok), 0)
    weight = jnp.zeros((slots, tok), jnp.float32)
    for k in range(slot_ref.shape[0]):
        weight += jnp.where(here == slot_ref[k : k + 1, :], probs_ref[k : k + 1, :], 0.0)
    weight = weight.T.astype(jnp.bfloat16)
    tails_in(y_ref, xs, y_ref.shape[0] * MAIN)
    inner = 0.0
    for j in range(PARTS // 2):
        part = slice(j * span, (j + 1) * span)
        main_in(y_ref, xs, j)
        inner += dot(xs[:, part], cot_ref[:, part], ((1,), (1,)))
        mixed_ref[:, part] = dot(weight, xs[:, part]).astype(jnp.bfloat16)
    for k in range(slot_ref.shape[0]):
        mask = here == slot_ref[k : k + 1, :]
        grads_ref[k : k + 1, :] = jnp.sum(jnp.where(mask, inner, 0.0), axis=0, keepdims=True)


def combine(slot_t, probs_t, cotangent, y):
    model = cotangent.shape[1]
    return pl.pallas_call(
        combine_kernel,
        out_shape=[
            jax.ShapeDtypeStruct(cotangent.shape, jnp.bfloat16),
            jax.ShapeDtypeStruct(probs_t.shape, jnp.float32),
        ],
        scratch_shapes=[pltpu.VMEM((y.shape[0] * CAP, model), jnp.bfloat16)],
        compiler_params=pltpu.CompilerParams(vmem_limit_bytes=40 * MIB),
    )(slot_t, probs_t, cotangent, y)


def exchange(messages):
    return lax.all_to_all(messages, ("node", "local"), split_axis=0, concat_axis=0, tiled=True)


def per_device(tokens, expert_ids, route_probs, cotangent, gate_weight, up_weight, down_weight):
    devices = lax.axis_size("node") * lax.axis_size("local")
    packed, slot_t = pack(expert_ids.T, tokens, devices)
    received = exchange(packed)
    results = expert_apply(received, gate_weight[0], up_weight[0], down_weight[0])
    returned = exchange(results)
    mixed, grads_t = combine(slot_t, route_probs.T, cotangent, returned)
    return mixed, grads_t.T


def solution(mesh):
    placed = (P(("node", "local"), None),) * 4 + (P(("node", "local"), None, None),) * 3
    return jax.shard_map(
        per_device,
        mesh=mesh,
        in_specs=placed,
        out_specs=(P(("node", "local"), None), P(("node", "local"), None)),
        check_vma=False,
    )
```

time: 321 us -> 304 us (0.947)
  Pallas kernels: 56.5 us -> 39.9 us
    pallas_call x2, Pallas kernels: 46.3 us -> 33.1 us  [the longest x1 28.9 us: expert_apply(): pl.pallas_call(expert_kernel, grid=(x.shape[0] // messages,), in_specs=[b...]
    pallas_call x1, Pallas kernels: 10.1 us -> 6.78 us  [combine(): pl.pallas_call(combine_kernel, out_shape=[jax.ShapeDtypeStruct(cotangent....]
where the time goes in v3:
time: 304 us; the launch traced here: 299 us
  blocking collectives  256 us (84%)
  Pallas kernels  39.9 us (13%)
    all_to_all x2, blocking collectives, exchange(): lax.all_to_all(messages, ('node', 'local'), split_axis=0, concat_axis=0,...  256 us
    pallas_call x1, Pallas kernels, expert_apply(): pl.pallas_call(expert_kernel, grid=(x.shape[0] // messages,), in_specs=[b...  28.9 us
    pallas_call x1, Pallas kernels, combine(): pl.pallas_call(combine_kernel, out_shape=[jax.ShapeDtypeStruct(cotangent....  6.78 us

profile of v3, /device:TPU:66, one launch (start us, length us, event | category | flops | bytes accessed | tf_op | source)
XLA Modules:
  0.0 298.9 jit_solution(12042635795242880220)
XLA Ops:
  0.6 0.0 copy-start.2
  0.6 1.2 copy-done.2
  1.9 0.0 copy-start.4
  1.9 0.7 copy-done.4
  2.5 0.0 slice-start
  2.5 0.0 slice-start.2
  2.5 4.2 %shard_map.86 = (bf16[128,80,512]{2,1,0:T(8,128)(2,1)S(1)}, s32[8,128]{1,0:T(8,128)S(1)}) custom-call(s32[8,128]{1,0:T(8,128)S(1)} %bitcast.14, bf16[128,4096]{1,0:T(8,128)(2,1)S(1)} %copy-done.2), custom_call_target="tpu_custom_call" | custom-call | tf_op jit(solution)/shard_map/pallas_call | solution.py:116
  6.8 0.0 slice-start.1
  6.8 0.0 slice-start.3
  6.8 0.0 copy-start
  6.8 128.1 %all_to_all.10.x_ref = bf16[128,80,512]{2,1,0:T(8,128)(2,1)} all-to-all(bf16[128,80,512]{2,1,0:T(8,128)(2,1)S(1)} %get-tuple-element.7), channel_id=1, replica_groups=mesh['node'=16,'local'=8] {'node','local'}, dimensions={0} | all-to-all | bytes 20971520 | tf_op jit(solution)/shard_map/all_to_all | solution.py:211
  134.9 0.0 slice-done
  134.9 0.0 slice-done.2
  134.9 0.0 slice-done.1
  134.9 0.0 slice-done.3
  134.9 0.0 copy-done
  134.9 28.9 %shard_map.87 = bf16[128,80,512]{2,1,0:T(8,128)(2,1)S(1)} custom-call(bf16[128,80,512]{2,1,0:T(8,128)(2,1)} %all_to_all.10.x_ref, bf16[4096,768]{1,0:T(8,128)(2,1)S(1)} %bitcast.8, bf16[4096,768]{1,0:T(8,128)(2,1)S(1)} %bitcast.11, bf16[768,4096]{1,0:T(8,128)(2,1)S(1)} %bitcast.12), custom_call_target="tpu_custom_call" | custom-call | tf_op jit(solution)/shard_map/pallas_call | solution.py:162
  163.8 0.0 copy-start.1
  163.8 0.0 copy-start.3
  163.8 128.2 %all_to_all.11.y_ref = bf16[128,80,512]{2,1,0:T(8,128)(2,1)S(1)} all-to-all(bf16[128,80,512]{2,1,0:T(8,128)(2,1)S(1)} %shard_map.87), channel_id=1, replica_groups=mesh['node'=16,'local'=8] {'node','local'}, dimensions={0} | all-to-all | bytes 20971520 | tf_op jit(solution)/shard_map/all_to_all | solution.py:211
  292.1 0.0 copy-done.1
  292.1 0.0 copy-done.3
  292.1 6.8 %shard_map.88 = (bf16[128,4096]{1,0:T(8,128)(2,1)}, f32[8,128]{1,0:T(8,128)}) custom-call(s32[8,128]{1,0:T(8,128)S(1)} %get-tuple-element.6.slot_ref, f32[8,128]{1,0:T(8,128)S(1)} %bitcast.13, bf16[128,4096]{1,0:T(8,128)(2,1)S(1)} %copy-done.1, bf16[128,80,512]{2,1,0:T(8,128)(2,1)S(1)} %all_to_all.11.y_ref), custom_call_target="tpu_custom_call" | custom-call | tf_op jit(solution)/shard_map/pallas_call | solution.py:199
  (2 shorter events, 0.0 us)
Async XLA Ops:
  0.6 1.2 copy-start.2
  1.9 0.7 copy-start.4
  2.5 132.3 %slice-start = ((s8[6291456]{0:T(1024)(128)(4,1)}), s8[4194304]{0:T(1024)(128)(4,1)S(1)}, s32[]{:S(2)}) async-start(s8[6291456]{0:T(1024)(128)(4,1)} %bitcast.6), calls=%async_computation.2 | async-start | bytes 8388608
  2.5 132.3 %slice-start.2 = ((s8[6291456]{0:T(1024)(128)(4,1)}), s8[2097152]{0:T(1024)(128)(4,1)S(1)}, s32[]{:S(2)}) async-start(s8[6291456]{0:T(1024)(128)(4,1)} %bitcast.9), calls=%async_computation.4 | async-start | bytes 4194304
  6.8 128.1 %slice-start.1 = ((s8[6291456]{0:T(1024)(128)(4,1)}), s8[2097152]{0:T(1024)(128)(4,1)S(1)}, s32[]{:S(2)}) async-start(s8[6291456]{0:T(1024)(128)(4,1)} %bitcast.6), calls=%async_computation.3 | async-start | bytes 4194304
  6.8 128.1 %slice-start.3 = ((s8[6291456]{0:T(1024)(128)(4,1)}), s8[4194304]{0:T(1024)(128)(4,1)S(1)}, s32[]{:S(2)}) async-start(s8[6291456]{0:T(1024)(128)(4,1)} %bitcast.9), calls=%async_computation.5 | async-start | bytes 8388608
  6.8 128.1 %copy-start = (bf16[1,768,4096]{2,1,0:T(8,128)(2,1)S(1)}, bf16[1,768,4096]{2,1,0:T(8,128)(2,1)}, u32[]{:S(2)}) copy-start(bf16[1,768,4096]{2,1,0:T(8,128)(2,1)} %param.13) | copy-start | bytes 18874372
  163.8 128.3 %copy-start.1 = (bf16[128,4096]{1,0:T(8,128)(2,1)S(1)}, bf16[128,4096]{1,0:T(8,128)(2,1)}, u32[]{:S(2)}) copy-start(bf16[128,4096]{1,0:T(8,128)(2,1)} %cot_ref.1) | copy-start | bytes 3145732
  163.8 128.2 %copy-start.3 = (f32[128,8]{0,1:T(8,128)S(1)}, f32[128,8]{0,1:T(8,128)}, u32[]{:S(2)}) copy-start(f32[128,8]{0,1:T(8,128)} %param.9) | copy-start | bytes 12292

commit v4 on v3

--- a/solution.py
+++ b/solution.py
@@ -26,14 +26,14 @@
     return lax.dot_general(a, b, (dims, ((), ())), preferred_element_type=jnp.float32)
 
 
-def tails_in(x_ref, xs, base):
+def tails_in(x_ref, first, xs, base):
     width = x_ref.shape[2]
     slots = SUB // PARTS
     out, src = iota((SUB, SUB), 0), iota((SUB, SUB), 1)
     order = (src == (out % slots) * PARTS + out // slots).astype(jnp.bfloat16)
     per = SUB // TILE
     for b in range(x_ref.shape[0] // per):
-        rows = x_ref[b * per : (b + 1) * per, BODY:ROWS, :].reshape(SUB, width)
+        rows = x_ref[b * per : (b + 1) * per, first : first + TILE, :].reshape(SUB, width)
         rows = dot(order, rows).astype(jnp.bfloat16)
         for q in range(PARTS):
             xs[base + b * slots : base + (b + 1) * slots, q * width : (q + 1) * width] = rows[q * slots : (q + 1) * slots, :]
@@ -48,7 +48,7 @@
     for b in range(out_ref.shape[0] // per):
         rows = [tails[b * slots : (b + 1) * slots, q * width : (q + 1) * width] for q in range(PARTS)]
         rows = dot(order, jnp.concatenate(rows, axis=0)).astype(jnp.bfloat16)
-        out_ref[b * per : (b + 1) * per, BODY:ROWS, :] = rows.reshape(per, TILE, width)
+        out_ref[b * per : (b + 1) * per, :, :] = rows.reshape(per, TILE, width)
 
 
 def main_in(x_ref, xs, j, step=32):
@@ -67,10 +67,10 @@
     out_ref[:, j * TILE : (j + 1) * TILE, :] = jnp.concatenate(halves, axis=1).astype(jnp.bfloat16)
 
 
-def pack_kernel(experts, ids_ref, tokens_ref, out_ref, slot_ref, place, tails):
+def pack_kernel(experts, ids_ref, tokens_ref, body_ref, tail_ref, slot_ref, place, tails):
     step = pl.program_id(0)
     tok, model = tokens_ref.shape
-    group = out_ref.shape[0]
+    group = body_ref.shape[0]
     span = model // PARTS * 2
 
     @pl.when(step == 0)
@@ -105,14 +105,14 @@
     for j in range(PARTS // 2):
         part = slice(j * span, (j + 1) * span)
         tails[:, part] = dot(late, tokens_ref[:, part]).astype(jnp.bfloat16)
-        main_out(dot(main, tokens_ref[:, part]), out_ref, j)
-    tails_out(tails, out_ref)
+        main_out(dot(main, tokens_ref[:, part]), body_ref, j)
+    tails_out(tails, tail_ref)
 
 
 def pack(ids_t, tokens, experts):
     tok, model = tokens.shape
     group = 32
-    shape = (ROWS, model // PARTS)
+    width = model // PARTS
     return pl.pallas_call(
         functools.partial(pack_kernel, experts),
         grid=(experts // group,),
@@ -121,11 +121,13 @@
             pl.BlockSpec(tokens.shape, lambda i: (0, 0)),
         ],
         out_specs=[
-            pl.BlockSpec((group, *shape), lambda i: (i, 0, 0)),
+            pl.BlockSpec((group, BODY, width), lambda i: (i, 0, 0)),
+            pl.BlockSpec((group, TILE, width), lambda i: (i, 0, 0)),
             pl.BlockSpec(ids_t.shape, lambda i: (0, 0)),
         ],
         out_shape=[
-            jax.ShapeDtypeStruct((experts, *shape), jnp.bfloat16),
+            jax.ShapeDtypeStruct((experts, BODY, width), jnp.bfloat16),
+            jax.ShapeDtypeStruct((experts, TILE, width), jnp.bfloat16),
             jax.ShapeDtypeStruct(ids_t.shape, jnp.int32),
         ],
         scratch_shapes=[
@@ -136,41 +138,106 @@
     )(ids_t, tokens)
 
 
-def expert_kernel(x_ref, gate, up, down, y_ref, xs, tails):
-    main = x_ref.shape[0] * MAIN
-    model = gate.shape[0]
+def spans(model):
     span = model // PARTS * 2
-    tails_in(x_ref, xs, main)
+    return [slice(j * span, (j + 1) * span) for j in range(PARTS // 2)]
+
+
+def silu_product(gate_act, up_act):
+    return (gate_act / (1.0 + jnp.exp(-gate_act)) * up_act).astype(jnp.bfloat16)
+
+
+def fetches(held, given, sems):
+    gate, up, down = held
+    copies = []
+    for j, part in enumerate(spans(gate.shape[0])):
+        copies.append(pltpu.make_async_copy(given[0].at[part, :], gate.at[part, :], sems.at[0, j]))
+        copies.append(pltpu.make_async_copy(given[1].at[part, :], up.at[part, :], sems.at[1, j]))
+    for j, part in enumerate(spans(gate.shape[0])):
+        copies.append(pltpu.make_async_copy(given[2].at[:, part], down.at[:, part], sems.at[2, j]))
+    return copies
+
+
+def held_weights(gate, up, down):
+    return [pltpu.VMEM(w.shape, w.dtype) for w in (gate, up, down)] + [pltpu.SemaphoreType.DMA((3, PARTS // 2))]
+
+
+def main_kernel(x_ref, gate_in, up_in, down_in, y_ref, xs, gate, up, down, sems):
+    copies = fetches((gate, up, down), (gate_in, up_in, down_in), sems)
+
+    def first(act, some):
+        @pl.when(pl.program_id(0) == 0)
+        def _():
+            for copy in some:
+                act(copy)
+
+    first(lambda copy: copy.start(), copies)
+    first(lambda copy: copy.wait(), copies[: PARTS // 2])
     gate_act, up_act = 0.0, 0.0
-    for j in range(PARTS // 2):
-        part = slice(j * span, (j + 1) * span)
+    for j, part in enumerate(spans(gate.shape[0])):
         main_in(x_ref, xs, j)
+        if 2 * j == PARTS // 2:
+            first(lambda copy: copy.wait(), copies[PARTS // 2 : PARTS])
         gate_act += dot(xs[:, part], gate[part, :])
         up_act += dot(xs[:, part], up[part, :])
-    hidden = (gate_act / (1.0 + jnp.exp(-gate_act)) * up_act).astype(jnp.bfloat16)
-    for j in range(PARTS // 2):
-        part = slice(j * span, (j + 1) * span)
-        result = dot(hidden, down[:, part])
-        main_out(result[:main], y_ref, j)
-        tails[:, part] = result[main:].astype(jnp.bfloat16)
-    tails_out(tails, y_ref)
-
-
-def expert_apply(x, gate, up, down, messages=32):
-    model = gate.shape[0]
-    block = pl.BlockSpec((messages, *x.shape[1:]), lambda i: (i, 0, 0))
+    hidden = silu_product(gate_act, up_act)
+    first(lambda copy: copy.wait(), copies[PARTS:])
+    for j, part in enumerate(spans(gate.shape[0])):
+        main_out(dot(hidden, down[:, part]), y_ref, j)
+
+
+def main_apply(x, gate, up, down, messages=32):
+    count, _, width = x.shape
+    model, ff = gate.shape
+    block = pl.BlockSpec((messages, BODY, width), lambda i: (i, 0, 0))
     return pl.pallas_call(
-        expert_kernel,
-        grid=(x.shape[0] // messages,),
-        in_specs=[block] + [pl.BlockSpec(memory_space=pltpu.VMEM)] * 3,
+        main_kernel,
+        grid=(count // messages,),
+        in_specs=[block] + [pl.BlockSpec(memory_space=pltpu.HBM)] * 3,
         out_specs=block,
-        out_shape=jax.ShapeDtypeStruct(x.shape, jnp.bfloat16),
-        scratch_shapes=[
-            pltpu.VMEM((messages * CAP, model), jnp.bfloat16),
-            pltpu.VMEM((messages * TAIL, model), jnp.bfloat16),
-        ],
-        compiler_params=pltpu.CompilerParams(vmem_limit_bytes=24 * MIB),
+        out_shape=jax.ShapeDtypeStruct((count, ROWS, width), jnp.bfloat16),
+        scratch_shapes=[pltpu.VMEM((messages * MAIN, model), jnp.bfloat16)] + held_weights(gate, up, down),
+        compiler_params=pltpu.CompilerParams(vmem_limit_bytes=50 * MIB),
+        cost_estimate=pl.CostEstimate(
+            flops=6 * count * MAIN * model * ff, bytes_accessed=4 * x.size, transcendentals=count * MAIN * ff
+        ),
     )(x, gate, up, down)
+
+
+def tail_kernel(x_ref, gate_in, up_in, down_in, _, y_ref, xs, gate, up, down, sems):
+    copies = fetches((gate, up, down), (gate_in, up_in, down_in), sems)
+    for copy in copies:
+        copy.start()
+    tails_in(x_ref, 0, xs, 0)
+    gate_act, up_act = 0.0, 0.0
+    for j, part in enumerate(spans(gate.shape[0])):
+        copies[2 * j].wait()
+        copies[2 * j + 1].wait()
+        gate_act += dot(xs[:, part], gate[part, :])
+        up_act += dot(xs[:, part], up[part, :])
+    hidden = silu_product(gate_act, up_act)
+    for j, part in enumerate(spans(gate.shape[0])):
+        copies[PARTS + j].wait()
+        xs[:, part] = dot(hidden, down[:, part]).astype(jnp.bfloat16)
+    tails_out(xs, y_ref)
+
+
+def tail_apply(x, gate, up, down, messages):
+    count, _, width = x.shape
+    model, ff = gate.shape
+    return pl.pallas_call(
+        tail_kernel,
+        grid=(1,),
+        in_specs=[pl.BlockSpec(x.shape, lambda i: (0, 0, 0))] + [pl.BlockSpec(memory_space=pltpu.HBM)] * 4,
+        out_specs=pl.BlockSpec(x.shape, lambda i: (0, BODY // TILE, 0)),
+        out_shape=jax.ShapeDtypeStruct(messages.shape, jnp.bfloat16),
+        scratch_shapes=[pltpu.VMEM((count * TAIL, model), jnp.bfloat16)] + held_weights(gate, up, down),
+        input_output_aliases={4: 0},
+        compiler_params=pltpu.CompilerParams(vmem_limit_bytes=50 * MIB),
+        cost_estimate=pl.CostEstimate(
+            flops=6 * count * TAIL * model * ff, bytes_accessed=4 * x.size, transcendentals=count * TAIL * ff
+        ),
+    )(x, gate, up, down, messages)
 
 
 def combine_kernel(slot_ref, probs_ref, cot_ref, y_ref, mixed_ref, grads_ref, xs):
@@ -182,7 +249,7 @@
     for k in range(slot_ref.shape[0]):
         weight += jnp.where(here == slot_ref[k : k + 1, :], probs_ref[k : k + 1, :], 0.0)
     weight = weight.T.astype(jnp.bfloat16)
-    tails_in(y_ref, xs, y_ref.shape[0] * MAIN)
+    tails_in(y_ref, BODY, xs, y_ref.shape[0] * MAIN)
     inner = 0.0
     for j in range(PARTS // 2):
         part = slice(j * span, (j + 1) * span)
@@ -213,9 +280,12 @@
 
 def per_device(tokens, expert_ids, route_probs, cotangent, gate_weight, up_weight, down_weight):
     devices = lax.axis_size("node") * lax.axis_size("local")
-    packed, slot_t = pack(expert_ids.T, tokens, devices)
-    received = exchange(packed)
-    results = expert_apply(received, gate_weight[0], up_weight[0], down_weight[0])
+    body, tail, slot_t = pack(expert_ids.T, tokens, devices)
+    weights = gate_weight[0], up_weight[0], down_weight[0]
+    body = exchange(body)
+    body, tail = lax.optimization_barrier((body, tail))
+    tail = exchange(tail)
+    results = tail_apply(tail, *weights, main_apply(body, *weights))
     returned = exchange(results)
     mixed, grads_t = combine(slot_t, route_probs.T, cotangent, returned)
     return mixed, grads_t.T

time: 304 us -> 301 us (level)
  blocking collectives: 256 us -> 233 us
  starting transfers between devices: 0 us -> 10.7 us
  Pallas kernels: 39.9 us -> 49.7 us
    all_to_all x2, blocking collectives: 256 us -> 233 us  [exchange(): lax.all_to_all(messages, ('node', 'local'), split_axis=0, concat_axis=0,...]
    all_to_all x0 -> x1, starting transfers between devices: none -> 10.7 us  [exchange(): lax.all_to_all(messages, ('node', 'local'), split_axis=0, concat_axis=0,...]
    pallas_call x1 -> x2, Pallas kernels: 28.9 us -> 38.7 us  [the longest x1 27.4 us: main_apply(): pl.pallas_call(main_kernel, grid=(count // messages,), in_specs=[block] +...]
  transfers between devices with their start and end apart: 0 -> 1, of which waited for: 0 -> 0; matrix products, arithmetic and copies ran while one was open for 0% -> 0% of each run, Pallas kernels for 0% -> 9%
where the time goes in v4:
time: 301 us; the launch traced here: 296 us
  blocking collectives  233 us (77%)
  Pallas kernels  49.7 us (17%)
  starting transfers between devices  10.7 us (4%)
    all_to_all x2, blocking collectives, exchange(): lax.all_to_all(messages, ('node', 'local'), split_axis=0, concat_axis=0,...  233 us
    pallas_call x1, Pallas kernels, main_apply(): pl.pallas_call(main_kernel, grid=(count // messages,), in_specs=[block] +...  27.4 us
    pallas_call x1, Pallas kernels, tail_apply(): pl.pallas_call(tail_kernel, grid=(1,), in_specs=[pl.BlockSpec(x.shape, la...  11.3 us
    all_to_all x1, starting transfers between devices, exchange(): lax.all_to_all(messages, ('node', 'local'), split_axis=0, concat_axis=0,...  10.7 us
    pallas_call x1, Pallas kernels, combine(): pl.pallas_call(combine_kernel, out_shape=[jax.ShapeDtypeStruct(cotangent....  6.79 us
  transfers between devices with their start and end apart: 1, of which 0 were waited for; matrix products, arithmetic and copies ran while one was open for 0% of the time, Pallas kernels for 9%

profile of v4, /device:TPU:66, one launch (start us, length us, event | category | flops | bytes accessed | tf_op | source)
XLA Modules:
  0.0 296.0 jit_solution(12831122526707104700)
XLA Ops:
  0.6 0.0 copy-start.2
  0.6 1.2 copy-done.2
  1.9 0.0 copy-start.4
  1.9 0.7 copy-done.4
  2.5 4.2 %shard_map.86 = (bf16[128,64,512]{2,1,0:T(8,128)(2,1)S(1)}, bf16[128,16,512]{2,1,0:T(8,128)(2,1)S(1)}, s32[8,128]{1,0:T(8,128)S(1)}) custom-call(s32[8,128]{1,0:T(8,128)S(1)} %bitcast.7, bf16[128,4096]{1,0:T(8,128)(2,1)S(1)} %copy-done.2), custom_call_target="tpu_custom_call" | custom-call | tf_op jit(solution)/shard_map/pallas_call | solution.py:116
  6.7 0.0 copy-start
  6.7 105.1 %all_to_all.15.x_ref = bf16[128,64,512]{2,1,0:T(8,128)(2,1)} all-to-all(bf16[128,64,512]{2,1,0:T(8,128)(2,1)S(1)} %get-tuple-element.10), channel_id=1, replica_groups=mesh['node'=16,'local'=8] {'node','local'}, dimensions={0} | all-to-all | bytes 16777216 | tf_op jit(solution)/shard_map/all_to_all | solution.py:278
  111.8 0.0 copy-done
  111.8 10.7 %all-to-all-start.1 = ((bf16[128,16,512]{2,1,0:T(8,128)(2,1)}), bf16[128,16,512]{2,1,0:T(8,128)(2,1)S(1)}, u32[]{:S(2)}, u32[]{:S(2)}) async-start(bf16[128,16,512]{2,1,0:T(8,128)(2,1)} %copy-done), calls=%async_computation.1 | async-start | bytes 4194304 | tf_op jit(solution)/shard_map/all_to_all | solution.py:278
  122.5 27.4 %shard_map.87._ = bf16[128,80,512]{2,1,0:T(8,128)(2,1)} custom-call(bf16[128,64,512]{2,1,0:T(8,128)(2,1)} %all_to_all.15.x_ref, bf16[4096,768]{1,0:T(8,128)(2,1)} %bitcast.8, bf16[4096,768]{1,0:T(8,128)(2,1)} %bitcast.10, bf16[768,4096]{1,0:T(8,128)(2,1)} %bitcast.12), custom_call_target="tpu_custom_call" | custom-call | flops 19327352832 | bytes 16777216 | tf_op jit(solution)/shard_map/pallas_call | solution.py:193
  150.0 0.0 all-to-all-done.1.x_ref
  150.0 11.3 %shard_map.88 = bf16[128,80,512]{2,1,0:T(8,128)(2,1)} custom-call(bf16[128,16,512]{2,1,0:T(8,128)(2,1)S(1)} %all-to-all-done.1.x_ref, bf16[4096,768]{1,0:T(8,128)(2,1)} %bitcast.9, bf16[4096,768]{1,0:T(8,128)(2,1)} %bitcast.11, bf16[768,4096]{1,0:T(8,128)(2,1)} %bitcast.13, bf16[128,80,512]{2,1,0:T(8,128)(2,1)} %shard_map.87._), custom_call_target="tpu_custom_call", output_to_operand_aliasing={{}: (4, {})} | custom-call | flops 4831838208 | bytes 4194304 | tf_op jit(solution)/shard_map/pallas_call | solution.py:228
  161.3 0.0 copy-start.1
  161.3 0.0 copy-start.3
  161.3 127.9 %all_to_all.16.y_ref = bf16[128,80,512]{2,1,0:T(8,128)(2,1)S(1)} all-to-all(bf16[128,80,512]{2,1,0:T(8,128)(2,1)} %shard_map.88), channel_id=1, replica_groups=mesh['node'=16,'local'=8] {'node','local'}, dimensions={0} | all-to-all | bytes 20971520 | tf_op jit(solution)/shard_map/all_to_all | solution.py:278
  289.2 0.0 copy-done.1
  289.2 0.0 copy-done.3
  289.2 6.8 %shard_map.89 = (bf16[128,4096]{1,0:T(8,128)(2,1)}, f32[8,128]{1,0:T(8,128)}) custom-call(s32[8,128]{1,0:T(8,128)S(1)} %get-tuple-element.9.slot_ref, f32[8,128]{1,0:T(8,128)S(1)} %bitcast.6, bf16[128,4096]{1,0:T(8,128)(2,1)S(1)} %copy-done.1, bf16[128,80,512]{2,1,0:T(8,128)(2,1)S(1)} %all_to_all.16.y_ref), custom_call_target="tpu_custom_call" | custom-call | tf_op jit(solution)/shard_map/pallas_call | solution.py:266
Async XLA Ops:
  0.6 1.2 copy-start.2
  1.9 0.7 copy-start.4
  6.7 105.1 %copy-start = (bf16[128,16,512]{2,1,0:T(8,128)(2,1)}, bf16[128,16,512]{2,1,0:T(8,128)(2,1)S(1)}, u32[]{:S(2)}) copy-start(bf16[128,16,512]{2,1,0:T(8,128)(2,1)S(1)} %get-tuple-element.12) | copy-start | bytes 6291460
  111.8 38.1 %all-to-all-start.1 = ((bf16[128,16,512]{2,1,0:T(8,128)(2,1)}), bf16[128,16,512]{2,1,0:T(8,128)(2,1)S(1)}, u32[]{:S(2)}, u32[]{:S(2)}) async-start(bf16[128,16,512]{2,1,0:T(8,128)(2,1)} %copy-done), calls=%async_computation.1 | async-start | bytes 4194304 | tf_op jit(solution)/shard_map/all_to_all | solution.py:278
  161.3 127.9 %copy-start.1 = (bf16[128,4096]{1,0:T(8,128)(2,1)S(1)}, bf16[128,4096]{1,0:T(8,128)(2,1)}, u32[]{:S(2)}) copy-start(bf16[128,4096]{1,0:T(8,128)(2,1)} %cot_ref.1) | copy-start | bytes 3145732
  161.3 127.9 %copy-start.3 = (f32[128,8]{0,1:T(8,128)S(1)}, f32[128,8]{0,1:T(8,128)}, u32[]{:S(2)}) copy-start(f32[128,8]{0,1:T(8,128)} %param.9) | copy-start | bytes 12292

commit v5 on v4

--- a/solution.py
+++ b/solution.py
@@ -67,7 +67,7 @@
     out_ref[:, j * TILE : (j + 1) * TILE, :] = jnp.concatenate(halves, axis=1).astype(jnp.bfloat16)
 
 
-def pack_kernel(experts, ids_ref, tokens_ref, body_ref, tail_ref, slot_ref, place, tails):
+def pack_kernel(experts, ids_in, tokens_in, body_ref, tail_ref, slot_ref, place, tails, ids_ref, tokens_ref, sems):
     step = pl.program_id(0)
     tok, model = tokens_ref.shape
     group = body_ref.shape[0]
@@ -75,6 +75,11 @@
 
     @pl.when(step == 0)
     def _():
+        ids_copy = pltpu.make_async_copy(ids_in, ids_ref, sems.at[0])
+        tokens_copy = pltpu.make_async_copy(tokens_in, tokens_ref, sems.at[1])
+        ids_copy.start()
+        tokens_copy.start()
+        ids_copy.wait()
         ids = ids_ref[...]
         expert = iota((experts, tok), 0)
         named = jnp.zeros((experts, tok), jnp.float32)
@@ -88,6 +93,7 @@
         for k in range(ids.shape[0]):
             chosen = expert == ids[k : k + 1, :]
             slot_ref[k : k + 1, :] = jnp.sum(jnp.where(chosen, slot_of, 0), axis=0, keepdims=True)
+        tokens_copy.wait()
 
     mine = place[pl.ds(pl.multiple_of(step * group, group), group), :]
     rank = iota((MAIN, tok), 0).astype(jnp.float32)
@@ -111,15 +117,13 @@
 
 def pack(ids_t, tokens, experts):
     tok, model = tokens.shape
+    ids_t, tokens = [pltpu.with_memory_space_constraint(a, pltpu.HBM) for a in (ids_t, tokens)]
     group = 32
     width = model // PARTS
     return pl.pallas_call(
         functools.partial(pack_kernel, experts),
         grid=(experts // group,),
-        in_specs=[
-            pl.BlockSpec(ids_t.shape, lambda i: (0, 0)),
-            pl.BlockSpec(tokens.shape, lambda i: (0, 0)),
-        ],
+        in_specs=[pl.BlockSpec(memory_space=pltpu.HBM)] * 2,
         out_specs=[
             pl.BlockSpec((group, BODY, width), lambda i: (i, 0, 0)),
             pl.BlockSpec((group, TILE, width), lambda i: (i, 0, 0)),
@@ -133,6 +137,9 @@
         scratch_shapes=[
             pltpu.VMEM((experts, tok), jnp.float32),
             pltpu.VMEM((group * TAIL, model), jnp.bfloat16),
+            pltpu.VMEM(ids_t.shape, jnp.int32),
+            pltpu.VMEM(tokens.shape, jnp.bfloat16),
+            pltpu.SemaphoreType.DMA((2,)),
         ],
         compiler_params=pltpu.CompilerParams(vmem_limit_bytes=14 * MIB),
     )(ids_t, tokens)

time: 301 us -> 300 us (level)
  no operation moved by 1% of the time
where the time goes in v5:
time: 300 us; the launch traced here: 295 us
  blocking collectives  233 us (78%)
  Pallas kernels  50.7 us (17%)
  starting transfers between devices  10.7 us (4%)
    all_to_all x2, blocking collectives, exchange(): lax.all_to_all(messages, ('node', 'local'), split_axis=0, concat_axis=0,...  233 us
    pallas_call x1, Pallas kernels, main_apply(): pl.pallas_call(main_kernel, grid=(count // messages,), in_specs=[block] +...  27.4 us
    pallas_call x1, Pallas kernels, tail_apply(): pl.pallas_call(tail_kernel, grid=(1,), in_specs=[pl.BlockSpec(x.shape, la...  11.3 us
    all_to_all x1, starting transfers between devices, exchange(): lax.all_to_all(messages, ('node', 'local'), split_axis=0, concat_axis=0,...  10.7 us
    pallas_call x1, Pallas kernels, combine(): pl.pallas_call(combine_kernel, out_shape=[jax.ShapeDtypeStruct(cotangent....  6.79 us
  transfers between devices with their start and end apart: 1, of which 0 were waited for; matrix products, arithmetic and copies ran while one was open for 0% of the time, Pallas kernels for 9%

profile of v5, /device:TPU:66, one launch (start us, length us, event | category | flops | bytes accessed | tf_op | source)
XLA Modules:
  0.0 295.1 jit_solution(14532422755039686614)
XLA Ops:
  0.6 5.2 %shard_map.86 = (bf16[128,64,512]{2,1,0:T(8,128)(2,1)S(1)}, bf16[128,16,512]{2,1,0:T(8,128)(2,1)S(1)}, s32[8,128]{1,0:T(8,128)S(1)}) custom-call(s32[8,128]{1,0:T(8,128)} %bitcast.13, bf16[128,4096]{1,0:T(8,128)(2,1)} %tokens_in.1), custom_call_target="tpu_custom_call" | custom-call | tf_op jit(solution)/shard_map/pallas_call | solution.py:123
  5.8 0.0 copy-start
  5.8 105.1 %all_to_all.15.x_ref = bf16[128,64,512]{2,1,0:T(8,128)(2,1)} all-to-all(bf16[128,64,512]{2,1,0:T(8,128)(2,1)S(1)} %get-tuple-element.10), channel_id=1, replica_groups=mesh['node'=16,'local'=8] {'node','local'}, dimensions={0} | all-to-all | bytes 16777216 | tf_op jit(solution)/shard_map/all_to_all | solution.py:285
  110.9 0.0 copy-done
  110.9 10.7 %all-to-all-start.1 = ((bf16[128,16,512]{2,1,0:T(8,128)(2,1)}), bf16[128,16,512]{2,1,0:T(8,128)(2,1)S(1)}, u32[]{:S(2)}, u32[]{:S(2)}) async-start(bf16[128,16,512]{2,1,0:T(8,128)(2,1)} %copy-done), calls=%async_computation.1 | async-start | bytes 4194304 | tf_op jit(solution)/shard_map/all_to_all | solution.py:285
  121.6 27.4 %shard_map.87._ = bf16[128,80,512]{2,1,0:T(8,128)(2,1)} custom-call(bf16[128,64,512]{2,1,0:T(8,128)(2,1)} %all_to_all.15.x_ref, bf16[4096,768]{1,0:T(8,128)(2,1)} %bitcast.7, bf16[4096,768]{1,0:T(8,128)(2,1)} %bitcast.9, bf16[768,4096]{1,0:T(8,128)(2,1)} %bitcast.11), custom_call_target="tpu_custom_call" | custom-call | flops 19327352832 | bytes 16777216 | tf_op jit(solution)/shard_map/pallas_call | solution.py:200
  149.1 0.0 all-to-all-done.1.x_ref
  149.1 11.3 %shard_map.88 = bf16[128,80,512]{2,1,0:T(8,128)(2,1)} custom-call(bf16[128,16,512]{2,1,0:T(8,128)(2,1)S(1)} %all-to-all-done.1.x_ref, bf16[4096,768]{1,0:T(8,128)(2,1)} %bitcast.8, bf16[4096,768]{1,0:T(8,128)(2,1)} %bitcast.10, bf16[768,4096]{1,0:T(8,128)(2,1)} %bitcast.12, bf16[128,80,512]{2,1,0:T(8,128)(2,1)} %shard_map.87._), custom_call_target="tpu_custom_call", output_to_operand_aliasing={{}: (4, {})} | custom-call | flops 4831838208 | bytes 4194304 | tf_op jit(solution)/shard_map/pallas_call | solution.py:235
  160.4 0.0 copy-start.1
  160.4 0.0 copy-start.2
  160.4 127.9 %all_to_all.16.y_ref = bf16[128,80,512]{2,1,0:T(8,128)(2,1)S(1)} all-to-all(bf16[128,80,512]{2,1,0:T(8,128)(2,1)} %shard_map.88), channel_id=1, replica_groups=mesh['node'=16,'local'=8] {'node','local'}, dimensions={0} | all-to-all | bytes 20971520 | tf_op jit(solution)/shard_map/all_to_all | solution.py:285
  288.3 0.0 copy-done.1
  288.3 0.0 copy-done.2
  288.3 6.8 %shard_map.89 = (bf16[128,4096]{1,0:T(8,128)(2,1)}, f32[8,128]{1,0:T(8,128)}) custom-call(s32[8,128]{1,0:T(8,128)S(1)} %get-tuple-element.9.slot_ref, f32[8,128]{1,0:T(8,128)S(1)} %bitcast.6, bf16[128,4096]{1,0:T(8,128)(2,1)S(1)} %copy-done.1, bf16[128,80,512]{2,1,0:T(8,128)(2,1)S(1)} %all_to_all.16.y_ref), custom_call_target="tpu_custom_call" | custom-call | tf_op jit(solution)/shard_map/pallas_call | solution.py:273
Async XLA Ops:
  5.8 105.1 %copy-start = (bf16[128,16,512]{2,1,0:T(8,128)(2,1)}, bf16[128,16,512]{2,1,0:T(8,128)(2,1)S(1)}, u32[]{:S(2)}) copy-start(bf16[128,16,512]{2,1,0:T(8,128)(2,1)S(1)} %get-tuple-element.12) | copy-start | bytes 6291460
  110.9 38.1 %all-to-all-start.1 = ((bf16[128,16,512]{2,1,0:T(8,128)(2,1)}), bf16[128,16,512]{2,1,0:T(8,128)(2,1)S(1)}, u32[]{:S(2)}, u32[]{:S(2)}) async-start(bf16[128,16,512]{2,1,0:T(8,128)(2,1)} %copy-done), calls=%async_computation.1 | async-start | bytes 4194304 | tf_op jit(solution)/shard_map/all_to_all | solution.py:285
  160.4 128.0 %copy-start.1 = (bf16[128,4096]{1,0:T(8,128)(2,1)S(1)}, bf16[128,4096]{1,0:T(8,128)(2,1)}, u32[]{:S(2)}) copy-start(bf16[128,4096]{1,0:T(8,128)(2,1)} %cot_ref.1) | copy-start | bytes 3145732
  160.4 127.9 %copy-start.2 = (f32[128,8]{0,1:T(8,128)S(1)}, f32[128,8]{0,1:T(8,128)}, u32[]{:S(2)}) copy-start(f32[128,8]{0,1:T(8,128)} %param.9) | copy-start | bytes 12292

commit v6 on v5

--- a/solution.py
+++ b/solution.py
@@ -169,7 +169,7 @@
     return [pltpu.VMEM(w.shape, w.dtype) for w in (gate, up, down)] + [pltpu.SemaphoreType.DMA((3, PARTS // 2))]
 
 
-def main_kernel(x_ref, gate_in, up_in, down_in, y_ref, xs, gate, up, down, sems):
+def main_kernel(x_ref, gate_in, up_in, down_in, slot_ref, probs_ref, y_ref, weight_ref, xs, gate, up, down, sems):
     copies = fetches((gate, up, down), (gate_in, up_in, down_in), sems)
 
     def first(act, some):
@@ -179,6 +179,16 @@
                 act(copy)
 
     first(lambda copy: copy.start(), copies)
+
+    @pl.when(pl.program_id(0) == 0)
+    def _():
+        tok, slots = weight_ref.shape
+        here = iota((slots, tok), 0)
+        weight = jnp.zeros((slots, tok), jnp.float32)
+        for k in range(slot_ref.shape[0]):
+            weight += jnp.where(here == slot_ref[k : k + 1, :], probs_ref[k : k + 1, :], 0.0)
+        weight_ref[...] = weight.T.astype(jnp.bfloat16)
+
     first(lambda copy: copy.wait(), copies[: PARTS // 2])
     gate_act, up_act = 0.0, 0.0
     for j, part in enumerate(spans(gate.shape[0])):
@@ -193,22 +203,27 @@
         main_out(dot(hidden, down[:, part]), y_ref, j)
 
 
-def main_apply(x, gate, up, down, messages=32):
+def main_apply(x, gate, up, down, slot_t, probs_t, messages=32):
     count, _, width = x.shape
     model, ff = gate.shape
     block = pl.BlockSpec((messages, BODY, width), lambda i: (i, 0, 0))
+    weight = (slot_t.shape[1], count * CAP)
+    whole = lambda shape: pl.BlockSpec(shape, lambda i: (0, 0))
     return pl.pallas_call(
         main_kernel,
         grid=(count // messages,),
-        in_specs=[block] + [pl.BlockSpec(memory_space=pltpu.HBM)] * 3,
-        out_specs=block,
-        out_shape=jax.ShapeDtypeStruct((count, ROWS, width), jnp.bfloat16),
+        in_specs=[block] + [pl.BlockSpec(memory_space=pltpu.HBM)] * 3 + [whole(slot_t.shape)] * 2,
+        out_specs=[block, whole(weight)],
+        out_shape=[
+            jax.ShapeDtypeStruct((count, ROWS, width), jnp.bfloat16),
+            jax.ShapeDtypeStruct(weight, jnp.bfloat16),
+        ],
         scratch_shapes=[pltpu.VMEM((messages * MAIN, model), jnp.bfloat16)] + held_weights(gate, up, down),
         compiler_params=pltpu.CompilerParams(vmem_limit_bytes=50 * MIB),
         cost_estimate=pl.CostEstimate(
             flops=6 * count * MAIN * model * ff, bytes_accessed=4 * x.size, transcendentals=count * MAIN * ff
         ),
-    )(x, gate, up, down)
+    )(x, gate, up, down, slot_t, probs_t)
 
 
 def tail_kernel(x_ref, gate_in, up_in, down_in, _, y_ref, xs, gate, up, down, sems):
@@ -247,15 +262,12 @@
     )(x, gate, up, down, messages)
 
 
-def combine_kernel(slot_ref, probs_ref, cot_ref, y_ref, mixed_ref, grads_ref, xs):
+def combine_kernel(slot_ref, weight_ref, cot_ref, y_ref, mixed_ref, grads_ref, xs):
     slots, model = xs.shape
     tok = cot_ref.shape[0]
     span = model // PARTS * 2
     here = iota((slots, tok), 0)
-    weight = jnp.zeros((slots, tok), jnp.float32)
-    for k in range(slot_ref.shape[0]):
-        weight += jnp.where(here == slot_ref[k : k + 1, :], probs_ref[k : k + 1, :], 0.0)
-    weight = weight.T.astype(jnp.bfloat16)
+    weight = weight_ref[...]
     tails_in(y_ref, BODY, xs, y_ref.shape[0] * MAIN)
     inner = 0.0
     for j in range(PARTS // 2):
@@ -268,17 +280,17 @@
         grads_ref[k : k + 1, :] = jnp.sum(jnp.where(mask, inner, 0.0), axis=0, keepdims=True)
 
 
-def combine(slot_t, probs_t, cotangent, y):
+def combine(slot_t, weight, cotangent, y):
     model = cotangent.shape[1]
     return pl.pallas_call(
         combine_kernel,
         out_shape=[
             jax.ShapeDtypeStruct(cotangent.shape, jnp.bfloat16),
-            jax.ShapeDtypeStruct(probs_t.shape, jnp.float32),
+            jax.ShapeDtypeStruct(slot_t.shape, jnp.float32),
         ],
         scratch_shapes=[pltpu.VMEM((y.shape[0] * CAP, model), jnp.bfloat16)],
         compiler_params=pltpu.CompilerParams(vmem_limit_bytes=40 * MIB),
-    )(slot_t, probs_t, cotangent, y)
+    )(slot_t, weight, cotangent, y)
 
 
 def exchange(messages):
@@ -292,9 +304,10 @@
     body = exchange(body)
     body, tail = lax.optimization_barrier((body, tail))
     tail = exchange(tail)
-    results = tail_apply(tail, *weights, main_apply(body, *weights))
+    messages, weight = main_apply(body, *weights, slot_t, route_probs.T)
+    results = tail_apply(tail, *weights, messages)
     returned = exchange(results)
-    mixed, grads_t = combine(slot_t, route_probs.T, cotangent, returned)
+    mixed, grads_t = combine(slot_t, weight, cotangent, returned)
     return mixed, grads_t.T
 
 

time: 300 us -> 300 us (level)
  no operation moved by 1% of the time
where the time goes in v6:
time: 300 us; the launch traced here: 295 us
  blocking collectives  233 us (78%)
  Pallas kernels  50.2 us (17%)
  starting transfers between devices  10.7 us (4%)
    all_to_all x2, blocking collectives, exchange(): lax.all_to_all(messages, ('node', 'local'), split_axis=0, concat_axis=0,...  233 us
    pallas_call x1, Pallas kernels, main_apply(): pl.pallas_call(main_kernel, grid=(count // messages,), in_specs=[block] +...  27.4 us
    pallas_call x1, Pallas kernels, tail_apply(): pl.pallas_call(tail_kernel, grid=(1,), in_specs=[pl.BlockSpec(x.shape, la...  11.4 us
    all_to_all x1, starting transfers between devices, exchange(): lax.all_to_all(messages, ('node', 'local'), split_axis=0, concat_axis=0,...  10.7 us
    pallas_call x1, Pallas kernels, combine(): pl.pallas_call(combine_kernel, out_shape=[jax.ShapeDtypeStruct(cotangent....  6.28 us
  transfers between devices with their start and end apart: 1, of which 0 were waited for; matrix products, arithmetic and copies ran while one was open for 0% of the time, Pallas kernels for 9%

profile of v6, /device:TPU:66, one launch (start us, length us, event | category | flops | bytes accessed | tf_op | source)
XLA Modules:
  0.0 294.6 jit_solution(11281293991987604124)
XLA Ops:
  0.6 5.2 %shard_map.86 = (bf16[128,64,512]{2,1,0:T(8,128)(2,1)S(1)}, bf16[128,16,512]{2,1,0:T(8,128)(2,1)S(1)}, s32[8,128]{1,0:T(8,128)S(1)}) custom-call(s32[8,128]{1,0:T(8,128)} %bitcast.13, bf16[128,4096]{1,0:T(8,128)(2,1)} %tokens_in.1), custom_call_target="tpu_custom_call" | custom-call | tf_op jit(solution)/shard_map/pallas_call | solution.py:123
  5.8 0.0 copy-start
  5.8 0.0 copy-start.2
  5.8 105.1 %all_to_all.15.x_ref = bf16[128,64,512]{2,1,0:T(8,128)(2,1)} all-to-all(bf16[128,64,512]{2,1,0:T(8,128)(2,1)S(1)} %get-tuple-element.12), channel_id=1, replica_groups=mesh['node'=16,'local'=8] {'node','local'}, dimensions={0} | all-to-all | bytes 16777216 | tf_op jit(solution)/shard_map/all_to_all | solution.py:297
  110.9 0.0 copy-done
  110.9 10.7 %all-to-all-start.1 = ((bf16[128,16,512]{2,1,0:T(8,128)(2,1)}), bf16[128,16,512]{2,1,0:T(8,128)(2,1)S(1)}, u32[]{:S(2)}, u32[]{:S(2)}) async-start(bf16[128,16,512]{2,1,0:T(8,128)(2,1)} %copy-done), calls=%async_computation.1 | async-start | bytes 4194304 | tf_op jit(solution)/shard_map/all_to_all | solution.py:297
  121.6 0.0 copy-done.2
  121.7 27.4 %shard_map.87 = (bf16[128,80,512]{2,1,0:T(8,128)(2,1)}, bf16[128,1280]{1,0:T(8,128)(2,1)S(1)}) custom-call(bf16[128,64,512]{2,1,0:T(8,128)(2,1)} %all_to_all.15.x_ref, bf16[4096,768]{1,0:T(8,128)(2,1)} %bitcast.7, bf16[4096,768]{1,0:T(8,128)(2,1)} %bitcast.9, bf16[768,4096]{1,0:T(8,128)(2,1)} %bitcast.11, s32[8,128]{1,0:T(8,128)S(1)} %get-tuple-element.11.slot_ref, ...), custom_call_target="tpu_custom_call" | custom-call | flops 19327352832 | bytes 16777216 | tf_op jit(solution)/shard_map/pallas_call | solution.py:212
  149.0 0.0 all-to-all-done.1.x_ref
  149.0 11.4 %shard_map.88 = bf16[128,80,512]{2,1,0:T(8,128)(2,1)} custom-call(bf16[128,16,512]{2,1,0:T(8,128)(2,1)S(1)} %all-to-all-done.1.x_ref, bf16[4096,768]{1,0:T(8,128)(2,1)} %bitcast.8, bf16[4096,768]{1,0:T(8,128)(2,1)} %bitcast.10, bf16[768,4096]{1,0:T(8,128)(2,1)} %bitcast.12, bf16[128,80,512]{2,1,0:T(8,128)(2,1)} %get-tuple-element.17._), custom_call_target="tpu_custom_call", output_to_operand_aliasing={{}: (4, {})} | custom-call | flops 4831838208 | bytes 4194304 | tf_op jit(solution)/shard_map/pallas_call | solution.py:250
  160.4 0.0 copy-start.1
  160.4 127.9 %all_to_all.16.y_ref = bf16[128,80,512]{2,1,0:T(8,128)(2,1)S(1)} all-to-all(bf16[128,80,512]{2,1,0:T(8,128)(2,1)} %shard_map.88), channel_id=1, replica_groups=mesh['node'=16,'local'=8] {'node','local'}, dimensions={0} | all-to-all | bytes 20971520 | tf_op jit(solution)/shard_map/all_to_all | solution.py:297
  288.3 0.0 copy-done.1
  288.3 6.3 %shard_map.89 = (bf16[128,4096]{1,0:T(8,128)(2,1)}, f32[8,128]{1,0:T(8,128)}) custom-call(s32[8,128]{1,0:T(8,128)S(1)} %get-tuple-element.11.slot_ref, bf16[128,1280]{1,0:T(8,128)(2,1)S(1)} %get-tuple-element.15.weight_ref, bf16[128,4096]{1,0:T(8,128)(2,1)S(1)} %copy-done.1, bf16[128,80,512]{2,1,0:T(8,128)(2,1)S(1)} %all_to_all.16.y_ref), custom_call_target="tpu_custom_call" | custom-call | tf_op jit(solution)/shard_map/pallas_call | solution.py:285
Async XLA Ops:
  5.8 105.1 %copy-start = (bf16[128,16,512]{2,1,0:T(8,128)(2,1)}, bf16[128,16,512]{2,1,0:T(8,128)(2,1)S(1)}, u32[]{:S(2)}) copy-start(bf16[128,16,512]{2,1,0:T(8,128)(2,1)S(1)} %get-tuple-element.16) | copy-start | bytes 6291460
  5.8 115.8 %copy-start.2 = (f32[128,8]{0,1:T(8,128)S(1)}, f32[128,8]{0,1:T(8,128)}, u32[]{:S(2)}) copy-start(f32[128,8]{0,1:T(8,128)} %param.9) | copy-start | bytes 12292
  110.9 38.1 %all-to-all-start.1 = ((bf16[128,16,512]{2,1,0:T(8,128)(2,1)}), bf16[128,16,512]{2,1,0:T(8,128)(2,1)S(1)}, u32[]{:S(2)}, u32[]{:S(2)}) async-start(bf16[128,16,512]{2,1,0:T(8,128)(2,1)} %copy-done), calls=%async_computation.1 | async-start | bytes 4194304 | tf_op jit(solution)/shard_map/all_to_all | solution.py:297
  160.4 127.9 %copy-start.1 = (bf16[128,4096]{1,0:T(8,128)(2,1)S(1)}, bf16[128,4096]{1,0:T(8,128)(2,1)}, u32[]{:S(2)}) copy-start(bf16[128,4096]{1,0:T(8,128)(2,1)} %cot_ref.1) | copy-start | bytes 3145732
